TPU v7x, 32 devices: a whole 2x2x4 slice. The times are simulated.
32 devices in a mesh: team: 4 (over x, core), env: 8 (over z, y).
Axes of the slice: x: 2, y: 2, z: 4, core: 2. Of those that a mesh axis runs over, the one named last changes fastest.
Arguments:
- features: bfloat16 [16384, 512], P(('team', 'env')), may hold values from -7 to 7
- team_of: int32 [16384], P(('team', 'env')), may hold values from 0 to 3, as said below
- env_of: int32 [16384], P(('team', 'env')), may hold values from 0 to 63, as said below
- actions: int32 [16384], P(('team', 'env')), may hold values from 0 to 127
- old_logp: float32 [16384], P(('team', 'env')), as said below
- advantages: float32 [16384], P(('team', 'env')), may hold values from -4 to 9
- returns: bfloat16 [16384], P(('team', 'env')), may hold values from -4 to 4
- w_hidden: bfloat16 [512, 512], replicated, may hold values from -0.25 to 0.25
- w_comm: bfloat16 [512, 512], replicated, may hold values from -0.25 to 0.25
- w_policy: bfloat16 [512, 128], replicated, may hold values from -0.25 to 0.25
- norm_gain: float32 [512], replicated, may hold values from 0.5 to 1.5
- w_query: bfloat16 [512, 512], replicated, may hold values from -0.25 to 0.25
- w_key: bfloat16 [512, 512], replicated, may hold values from -0.25 to 0.25
- w_value: float32 [512], replicated, may hold values from -0.25 to 0.25
Outputs:
- grad_input: bfloat16 [16384, 512], P(('team', 'env'))
- grad_w_hidden: float32 [512, 512], P(('team', 'env'))
- grad_w_comm: float32 [512, 512], P(('team', 'env'))
- grad_w_policy: float32 [512, 128], P(('team', 'env'))
- grad_w_query: float32 [512, 512], P(('team', 'env'))
- grad_w_key: float32 [512, 512], P(('team', 'env'))
Inputs may be any that keep to these rules, and one draw needn't show every extreme that they name: `team_of`: rows form 4 * 8 blocks of 512, block b = t * 8 + e; over the blocks that share e, each team number names exactly 512 agents. `env_of`: block b = t * 8 + e of 512 rows holds exactly 32 agents of each environment (t * 8 + j) * 2 + l, 0 <= j < 8, 0 <= l < 2, and no others. `old_logp`: within 1.5 of -ln(128).
All inputs are finite; a program needn't handle non-finite values.
Results may differ from a plain program's by a relative error of at most 0.0077.
Values may be sent and summed in bfloat16 or wider, within the bound.
A program may use at most 64 MiB of HBM per device.

v0:
```python
import math

import jax
import jax.numpy as jnp
from jax import lax
from jax.sharding import PartitionSpec as P

HEADS = 4
TEAMS = 4
ENV_AGENTS = 256
ENV_DEV = 2


KL_WEIGHT = 0.5
NORM_EPS = 1e-05


def matmul(left_side, right_side):
    return jnp.dot(left_side, right_side, preferred_element_type=jnp.float32)


def times_trans(left_side, right_side):
    return lax.dot_general(
        left_side, right_side, (((1,), (1,)), ((), ())), preferred_element_type=jnp.float32
    )


def trans_times(left_side, right_side):
    return lax.dot_general(
        left_side, right_side, (((0,), (0,)), ((), ())), preferred_element_type=jnp.float32
    )


def normalize(values):
    center = values - jnp.mean(values, axis=-1, keepdims=True)
    spread = jnp.sqrt(jnp.mean(center * center, axis=-1, keepdims=True) + NORM_EPS)
    return (center / spread, spread)


def normalize_back(gradient, normed, spread):
    mean_grad = jnp.mean(gradient, axis=-1, keepdims=True)
    mean_along = jnp.mean(gradient * normed, axis=-1, keepdims=True)
    return (gradient - mean_grad - normed * mean_along) / spread


def critic_pass(inputs, targets, norm_gain, w_query, w_key, w_value, head_count):
    item_count, agent_count, model_width = inputs.shape
    head_width = model_width // head_count
    factor = 1.0 / math.sqrt(head_width)
    rows_in = inputs.astype(jnp.float32)
    input_hat, input_spread = normalize(rows_in)
    normed = (input_hat * norm_gain).astype(jnp.bfloat16)
    flat_shape = (item_count * agent_count, model_width)
    flat_normed = normed.reshape(flat_shape)
    query_rows = matmul(flat_normed, w_query).astype(jnp.bfloat16)
    key_rows = matmul(flat_normed, w_key).astype(jnp.bfloat16)
    head_shape = (item_count, agent_count, head_count, head_width)
    query_heads = query_rows.reshape(head_shape)
    key_heads = key_rows.reshape(head_shape)
    value_heads = normed.reshape(head_shape)
    scores = (
        jnp.einsum("cqhd,ckhd->chqk", query_heads, key_heads, preferred_element_type=jnp.float32)
        * factor
    )
    raised = jnp.exp(scores)
    attention = raised / jnp.sum(raised, axis=-1, keepdims=True)
    attention_low = attention.astype(jnp.bfloat16)
    attended = jnp.einsum(
        "chqk,ckhd->cqhd", attention_low, value_heads, preferred_element_type=jnp.float32
    )
    mixed = rows_in + attended.reshape(item_count, agent_count, model_width)
    mixed_hat, mixed_spread = normalize(mixed)
    value_out = jnp.sum(mixed_hat * w_value, axis=-1)
    value_grad = value_out - targets.astype(jnp.float32)
    mixed_grad = normalize_back(value_grad[..., None] * w_value, mixed_hat, mixed_spread)
    out_grad = mixed_grad.astype(jnp.bfloat16).reshape(head_shape)
    prob_grad = jnp.einsum(
        "cqhd,ckhd->chqk", out_grad, value_heads, preferred_element_type=jnp.float32
    )
    value_side = jnp.einsum(
        "chqk,cqhd->ckhd", attention_low, out_grad, preferred_element_type=jnp.float32
    )
    score_grad = (
        attention * (prob_grad - jnp.sum(attention * prob_grad, axis=-1, keepdims=True)) * factor
    )
    score_low = score_grad.astype(jnp.bfloat16)
    query_grad = jnp.einsum(
        "chqk,ckhd->cqhd", score_low, key_heads, preferred_element_type=jnp.float32
    ).astype(jnp.bfloat16)
    key_grad = jnp.einsum(
        "chqk,cqhd->ckhd", score_low, query_heads, preferred_element_type=jnp.float32
    ).astype(jnp.bfloat16)
    query_flat = query_grad.reshape(flat_shape)
    key_flat = key_grad.reshape(flat_shape)
    normed_grad = (
        times_trans(query_flat, w_query)
        + times_trans(key_flat, w_key)
        + value_side.reshape(flat_shape)
    )
    input_grad = mixed_grad + normalize_back(
        normed_grad.reshape(item_count, agent_count, model_width) * norm_gain,
        input_hat,
        input_spread,
    )
    return (input_grad.astype(jnp.bfloat16), flat_normed, query_flat, key_flat)


def body(
    features,
    team_of,
    env_of,
    actions,
    old_logp,
    advantages,
    returns,
    w_hidden,
    w_comm,
    w_policy,
    norm_gain,
    w_query,
    w_key,
    w_value,
):
    agent_rows, model_width = features.shape
    policy_width = w_policy.shape[1]
    team_devs = lax.axis_size("team")
    env_devs = lax.axis_size("env")
    devices_all = team_devs * env_devs
    members = team_devs * agent_rows // TEAMS
    inv_peers = 1.0 / (members - 1)
    team_mask = team_of[:, None] == jnp.arange(TEAMS, dtype=jnp.int32)[None, :]
    team_low = team_mask.astype(jnp.bfloat16)
    team_full = team_mask.astype(jnp.float32)
    team_sums = lax.psum(trans_times(team_low, features), "team")
    team_share = jnp.dot(
        team_full, team_sums, precision=lax.Precision.HIGHEST, preferred_element_type=jnp.float32
    )
    message = ((team_share - features.astype(jnp.float32)) * inv_peers).astype(jnp.bfloat16)
    advantage_total, advantage_squares = lax.psum(
        (jnp.sum(advantages), jnp.sum(advantages * advantages)), ("team", "env")
    )
    agent_total = agent_rows * devices_all
    advantage_mean = advantage_total / agent_total
    advantage_spread = advantage_squares / agent_total - advantage_mean * advantage_mean
    scaled_advantage = (advantages - advantage_mean) / jnp.sqrt(advantage_spread + NORM_EPS)
    pre_act = matmul(features, w_hidden) + matmul(message, w_comm)
    hidden = jnp.tanh(pre_act).astype(jnp.bfloat16)
    logits = matmul(hidden, w_policy)
    raised = jnp.exp(logits)
    totals = jnp.sum(raised, axis=-1, keepdims=True)
    probs_all = raised / totals
    log_probs = logits - jnp.log(totals)
    chosen = (actions[:, None] == jnp.arange(policy_width, dtype=jnp.int32)[None, :]).astype(
        jnp.float32
    )
    log_chosen = jnp.sum(chosen * log_probs, axis=-1)
    ratios = jnp.exp(log_chosen - old_logp)
    delta_grad = -ratios * scaled_advantage + KL_WEIGHT * (ratios - 1.0)
    logit_grad = (delta_grad[:, None] * (chosen - probs_all)).astype(jnp.bfloat16)
    per_peer = ENV_AGENTS // env_devs
    target_device = env_of // ENV_DEV % env_devs
    target_env = env_of % ENV_DEV
    ordering = jnp.argsort(target_env * env_devs + target_device, stable=True)
    inverse = jnp.argsort(ordering, stable=True)
    outgoing_rows = hidden[ordering].reshape(ENV_DEV, env_devs, per_peer, model_width)
    outgoing_targets = returns[ordering].reshape(ENV_DEV, env_devs, per_peer)
    arriving = lax.all_to_all(outgoing_rows, "env", split_axis=1, concat_axis=1, tiled=True)
    targets = lax.all_to_all(outgoing_targets, "env", split_axis=1, concat_axis=1, tiled=True)
    item_count = arriving.shape[0]
    input_grad, flat_normed, critic_query_flat, critic_key_flat = critic_pass(
        arriving.reshape(item_count, ENV_AGENTS, model_width),
        targets.reshape(item_count, ENV_AGENTS),
        norm_gain,
        w_query,
        w_key,
        w_value,
        HEADS,
    )
    returned = lax.all_to_all(
        input_grad.reshape(item_count, env_devs, per_peer, model_width),
        "env",
        split_axis=1,
        concat_axis=1,
        tiled=True,
    )
    stacked = (item_count, ENV_AGENTS, model_width)
    returned, normed_items, query_items, key_items = (
        returned,
        flat_normed.reshape(stacked),
        critic_query_flat.reshape(stacked),
        critic_key_flat.reshape(stacked),
    )
    flat_rows = (agent_rows, model_width)
    critic_grad = returned.reshape(flat_rows)[inverse]
    normed_flat = normed_items.reshape(flat_rows)
    query_flat = query_items.reshape(flat_rows)
    key_flat = key_items.reshape(flat_rows)
    hidden_grad = times_trans(logit_grad, w_policy) + critic_grad.astype(jnp.float32)
    hidden_full = hidden.astype(jnp.float32)
    pre_grad = (hidden_grad * (1.0 - hidden_full * hidden_full)).astype(jnp.bfloat16)
    message_grad = times_trans(pre_grad, w_comm)
    local_message = lax.dot_general(
        team_full,
        message_grad,
        (((0,), (0,)), ((), ())),
        precision=lax.Precision.HIGHEST,
        preferred_element_type=jnp.float32,
    )
    message_sums = lax.psum(local_message, "team")
    message_share = jnp.dot(
        team_full, message_sums, precision=lax.Precision.HIGHEST, preferred_element_type=jnp.float32
    )
    grad_input = (
        times_trans(pre_grad, w_hidden) + (message_share - message_grad) * inv_peers
    ).astype(jnp.bfloat16)
    pieces = [trans_times(features, pre_grad)]
    pieces.append(trans_times(message, pre_grad))
    pieces.append(trans_times(hidden, logit_grad))
    joined = lax.psum_scatter(
        jnp.concatenate(
            [
                jnp.concatenate(pieces, axis=1),
                jnp.concatenate(
                    [trans_times(normed_flat, query_flat), trans_times(normed_flat, key_flat)],
                    axis=1,
                ),
            ],
            axis=1,
        ),
        ("team", "env"),
        scatter_dimension=0,
        tiled=True,
    )
    actor_sums = joined[:, : joined.shape[1] - 2 * model_width]
    critic_sums = joined[:, joined.shape[1] - 2 * model_width :]
    grad_w_hidden = actor_sums[:, :model_width]
    grad_w_policy = actor_sums[:, actor_sums.shape[1] - policy_width :]
    grad_w_comm = actor_sums[:, model_width : 2 * model_width]
    grad_w_query = critic_sums[:, :model_width]
    grad_w_key = critic_sums[:, model_width:]
    return (grad_input, grad_w_hidden, grad_w_comm, grad_w_policy, grad_w_query, grad_w_key)


def solution(mesh):
    in_specs = (
        P(("team", "env"), None),
        P(("team", "env")),
        P(("team", "env")),
        P(("team", "env")),
        P(("team", "env")),
        P(("team", "env")),
        P(("team", "env")),
        P(),
        P(),
        P(),
        P(),
        P(),
        P(),
        P(),
    )
    out_specs = (
        P(("team", "env"), None),
        P(("team", "env"), None),
        P(("team", "env"), None),
        P(("team", "env"), None),
        P(("team", "env"), None),
        P(("team", "env"), None),
    )
    return jax.shard_map(body, mesh=mesh, in_specs=in_specs, out_specs=out_specs, check_vma=False)
```

profile of v0, /device:TPU:0, one launch (start us, length us, event | category | flops | bytes accessed | tf_op | source)
XLA Modules:
  0.0 329.4 jit_solution(13457157898700582570)
XLA Ops:
  8.0 3.8 %sort.31 = (s32[512]{0:T(512)}, s32[512]{0:T(512)S(1)}) sort(s32[512]{0:T(512)S(1)} %fusion.63, s32[512]{0:T(512)S(1)} %iota.15), dimensions={0}, to_apply=%region_7.8 | sort | flops 4608 | bytes 8192 | tf_op jit(solution)/shard_map/jit(argsort)/sort | solution.py:163
  11.8 3.6 %gather_fusion.1 = bf16[512]{0:T(512)(128)(2,1)S(1)} fusion(bf16[512]{0:T(512)(128)(2,1)} %param.20, s32[1024]{0:T(1024)S(1)} %pad_clamp_fusion.1), kind=kCustom, calls=%fused_computation.1 | custom fusion | bytes 4096 | tf_op jit(solution)/shard_map/gather | solution.py:166
  16.1 7.3 %all-to-all-start.1 = ((bf16[2,8,32]{2,0,1:T(2,128)(2,1)}), bf16[2,8,32]{2,0,1:T(2,128)(2,1)S(1)}, u32[]{:S(2)}, u32[]{:S(2)}) async-start(bf16[2,8,32]{2,0,1:T(2,128)(2,1)} %copy.121), calls=%async_computation.1 | async-start | bytes 8192 | tf_op jit(solution)/shard_map/all_to_all | solution.py:168
  24.8 6.7 %psum.28 = f32[4,512]{1,0:T(4,128)S(1)} all-reduce(f32[4,512]{1,0:T(4,128)S(1)} %fusion.56), channel_id=1, replica_groups=mesh['team'=4,'env'=8] {'team'}, use_global_device_ids=true, to_apply=%region_0.0 | all-reduce | flops 2048 | bytes 16384 | tf_op jit(solution)/shard_map/psum | solution.py:134
  34.1 2.0 gather_fusion
  36.9 5.4 %all-to-all-start = ((bf16[2,8,32,512]{3,2,0,1:T(8,128)(2,1)}), bf16[2,8,32,512]{3,2,0,1:T(8,128)(2,1)S(1)}, u32[]{:S(2)}, u32[]{:S(2)}) async-start(bf16[2,8,32,512]{3,2,0,1:T(8,128)(2,1)} %copy.114), calls=%async_computation | async-start | bytes 1048576 | tf_op jit(solution)/shard_map/all_to_all | solution.py:167
  43.0 42.2 %all-reduce = (f32[]{:T(128)}, f32[]{:T(128)}) all-reduce(f32[]{:T(128)} %get-tuple-element.43, f32[]{:T(128)} %get-tuple-element.42), channel_id=1, replica_groups=mesh['team'=4,'env'=8] {'team','env'}, use_global_device_ids=true, to_apply=%region_6.0 | all-reduce | flops 2 | bytes 16 | tf_op jit(solution)/shard_map/psum | solution.py:139
  85.2 3.8 %sort.32 = (s32[512]{0:T(512)}, s32[512]{0:T(512)S(1)}) sort(s32[512]{0:T(512)S(1)} %get-tuple-element.8, s32[512]{0:T(512)S(1)} %iota.16), dimensions={0}, to_apply=%region_19.20 | sort | flops 4608 | bytes 8192 | tf_op jit(solution)/shard_map/jit(argsort)/sort | solution.py:164
  91.5 2.1 copy.126
  107.8 5.6 %fusion.28 = bf16[2,256,4,128]{1,3,2,0:T(8,128)(2,1)} fusion(bf16[2,256,4,128]{1,3,2,0:T(8,128)(2,1)} %copy.129, f32[2,4,256,256]{2,3,1,0:T(8,128)} %fusion.53, f32[2,4,256,256]{2,3,1,0:T(8,128)} %copy-done.4, f32[2,4,256]{2,1,0:T(4,128)S(1)} %get-tuple-element.54), kind=kOutput, calls=%fused_computation.40 | convolution fusion | flops 139200768 | bytes 5251072 | tf_op jit(solution)/shard_map/chqk,cqhd->ckhd/dot_general | solution.py:90
  113.3 5.5 %fusion.31 = bf16[2,256,4,128]{1,3,2,0:T(8,128)(2,1)} fusion(bf16[2,256,4,128]{1,3,2,0:T(8,128)(2,1)} %copy.126, f32[2,4,256,256]{2,3,1,0:T(8,128)} %fusion.53, f32[2,4,256,256]{2,3,1,0:T(8,128)} %copy-done.4, f32[2,4,256]{2,1,0:T(4,128)S(1)} %get-tuple-element.54), kind=kOutput, calls=%fused_computation.41 | convolution fusion | flops 139200768 | bytes 5251072 | tf_op jit(solution)/shard_map/chqk,ckhd->cqhd/dot_general | solution.py:87
  118.8 3.3 %convolution_bitcast_fusion.1 = f32[2,256,4,128]{1,3,2,0:T(8,128)} fusion(f32[2,256]{1,0:T(2,128)S(1)} %get-tuple-element.60, f32[2,256]{1,0:T(2,128)S(1)} %get-tuple-element.61, f32[2,256]{1,0:T(2,128)S(1)} %sub.156, f32[4,128]{1,0:T(4,128)S(1)} %bitcast.94, f32[2,256]{1,0:T(2,128)S(1)} %add_sqrt_fusion.1, f32[2,256,4,128]{1,3,2,0:T(8,128)S(1)} %get-tuple-element.47, ...), kind=kOutput, calls=%fused_computation.30 | convolution fusion | flops 137887744 | bytes 4214784 | tf_op jit(solution)/shard_map/chqk,cqhd->ckhd/dot_general | solution.py:80
  122.5 2.2 copy.131
  127.5 2.6 copy.133
  130.1 3.1 multiply_reduce_fusion.6
  133.4 2.6 copy.123
  136.0 2.6 reshape.248
  138.6 3.0 multiply_convert_fusion.1
  142.4 4.7 %all-to-all-start.2 = ((bf16[2,8,32,512]{3,2,0,1:T(8,128)(2,1)}), bf16[2,8,32,512]{3,2,0,1:T(8,128)(2,1)S(1)}, u32[]{:S(2)}, u32[]{:S(2)}) async-start(bf16[2,8,32,512]{3,2,0,1:T(8,128)(2,1)} %copy.134), calls=%async_computation.2 | async-start | bytes 1048576 | tf_op jit(solution)/shard_map/all_to_all | solution.py:179
  150.9 9.1 %all-to-all-done.2 = bf16[2,8,32,512]{3,2,0,1:T(8,128)(2,1)S(1)} async-done(((bf16[2,8,32,512]{3,2,0,1:T(8,128)(2,1)}), bf16[2,8,32,512]{3,2,0,1:T(8,128)(2,1)S(1)}, u32[]{:S(2)}, u32[]{:S(2)}) %all-to-all-start.2) | async-done | bytes 524320 | tf_op jit(solution)/shard_map/all_to_all | solution.py:179
  160.1 2.0 gather_fusion.2
  170.0 5.8 %copy.146 = f32[512,2176]{1,0:T(8,128)} copy(f32[512,2176]{0,1:T(8,128)} %convolution_dynamic-update-slice_fusion) | data formatting | bytes 8912896
  178.0 5.7 %psum.31 = f32[4,512]{1,0:T(4,128)S(1)} all-reduce(f32[4,512]{1,0:T(4,128)S(1)} %fusion.55), channel_id=1, replica_groups=mesh['team'=4,'env'=8] {'team'}, use_global_device_ids=true, to_apply=%region_20.21 | all-reduce | flops 2048 | bytes 16384 | tf_op jit(solution)/shard_map/psum | solution.py:209
  185.7 134.1 %reduce-scatter.4.cloned.1.call-done = f32[16,2176]{1,0:T(8,128)} async-done(((f32[512,2176]{1,0:T(8,128)}), f32[16,2176]{1,0:T(8,128)}) %reduce-scatter.4.cloned.1.call-update) | async-done | bytes 139280
  (122 shorter events, 43.6 us)
Async XLA Ops:
  7.2 82.9 %copy-start = (bf16[512,512]{1,0:T(8,128)(2,1)S(1)}, bf16[512,512]{1,0:T(8,128)(2,1)}, u32[]{:S(2)}) copy-start(bf16[512,512]{1,0:T(8,128)(2,1)} %param.26) | copy-start | bytes 1572868
  7.2 26.0 %copy-start.1 = (bf16[512,512]{1,0:T(8,128)(2,1)S(1)}, bf16[512,512]{1,0:T(8,128)(2,1)}, u32[]{:S(2)}) copy-start(bf16[512,512]{1,0:T(8,128)(2,1)} %param.14) | copy-start | bytes 1572868
  7.2 26.0 %copy-start.8 = (bf16[512,512]{1,0:T(8,128)(2,1)S(1)}, bf16[512,512]{1,0:T(8,128)(2,1)}, u32[]{:S(2)}) copy-start(bf16[512,512]{1,0:T(8,128)(2,1)} %param.21) | copy-start | bytes 1572868
  15.4 18.2 %copy-start.6 = (bf16[512,512]{1,0:T(8,128)(2,1)S(1)}, bf16[512,512]{1,0:T(8,128)(2,1)}, u32[]{:S(2)}) copy-start(bf16[512,512]{1,0:T(8,128)(2,1)} %param.22) | copy-start | bytes 1572868
  16.1 20.8 %all-to-all-start.1 = ((bf16[2,8,32]{2,0,1:T(2,128)(2,1)}), bf16[2,8,32]{2,0,1:T(2,128)(2,1)S(1)}, u32[]{:S(2)}, u32[]{:S(2)}) async-start(bf16[2,8,32]{2,0,1:T(2,128)(2,1)} %copy.121), calls=%async_computation.1 | async-start | bytes 8192 | tf_op jit(solution)/shard_map/all_to_all | solution.py:168
  36.1 6.3 %copy-start.17 = (f32[512]{0:T(512)S(1)}, f32[512]{0:T(512)}, u32[]{:S(2)}) copy-start(f32[512]{0:T(512)} %param.19) | copy-start | bytes 6148
  36.1 53.8 %copy-start.16 = (f32[512]{0:T(512)S(1)}, f32[512]{0:T(512)}, u32[]{:S(2)}) copy-start(f32[512]{0:T(512)} %param.24) | copy-start | bytes 6148
  36.9 52.1 %all-to-all-start = ((bf16[2,8,32,512]{3,2,0,1:T(8,128)(2,1)}), bf16[2,8,32,512]{3,2,0,1:T(8,128)(2,1)S(1)}, u32[]{:S(2)}, u32[]{:S(2)}) async-start(bf16[2,8,32,512]{3,2,0,1:T(8,128)(2,1)} %copy.114), calls=%async_computation | async-start | bytes 1048576 | tf_op jit(solution)/shard_map/all_to_all | solution.py:167
  100.2 3.2 copy-start.12
  102.1 3.0 copy-start.4
  103.5 1.7 copy-start.15
  122.1 3.9 %copy-start.5 = (bf16[512,512]{1,0:T(8,128)(2,1)S(1)}, bf16[512,512]{1,0:T(8,128)(2,1)}, u32[]{:S(2)}) copy-start(bf16[512,512]{1,0:T(8,128)(2,1)} %param.25) | copy-start | bytes 1572868
  127.5 2.6 copy-start.10
  138.6 8.6 %copy-start.13 = (bf16[512,128]{1,0:T(8,128)(2,1)S(1)}, bf16[512,128]{1,0:T(8,128)(2,1)}, u32[]{:S(2)}) copy-start(bf16[512,128]{1,0:T(8,128)(2,1)} %param.23) | copy-start | bytes 393220
  141.6 8.6 %copy-start.18 = (s32[512]{0:T(512)S(1)}, s32[512]{0:T(512)}, u32[]{:S(2)}) copy-start(s32[512]{0:T(512)} %param.17) | copy-start | bytes 6148
  141.6 8.7 %copy-start.19 = (f32[512]{0:T(512)S(1)}, f32[512]{0:T(512)}, u32[]{:S(2)}) copy-start(f32[512]{0:T(512)} %param.18) | copy-start | bytes 6148
  142.4 17.6 %all-to-all-start.2 = ((bf16[2,8,32,512]{3,2,0,1:T(8,128)(2,1)}), bf16[2,8,32,512]{3,2,0,1:T(8,128)(2,1)S(1)}, u32[]{:S(2)}, u32[]{:S(2)}) async-start(bf16[2,8,32,512]{3,2,0,1:T(8,128)(2,1)} %copy.134), calls=%async_computation.2 | async-start | bytes 1048576 | tf_op jit(solution)/shard_map/all_to_all | solution.py:179
  147.2 172.6 %reduce-scatter.4.cloned.1.call-start = ((), (), s32[]{:S(2)}) async-start(), calls=%async_computation.4 | async-start | bytes 4595712
  160.1 2.0 copy-start.20
  162.1 1.0 copy-start.2
  164.6 2.5 copy-start.3
  166.0 2.4 copy-start.11
  175.8 1.0 copy-start.7
  177.5 6.9 %copy-start.9 = (bf16[512,512]{1,0:T(8,128)(2,1)S(1)}, bf16[512,512]{1,0:T(8,128)(2,1)}, u32[]{:S(2)}) copy-start(bf16[512,512]{1,0:T(8,128)(2,1)} %param.21) | copy-start | bytes 1572868
  (1 other events, 0.7 us)
Sparse Core Ops, SparseCore 0:
  175.9 143.8 reduce-scatter.3
where the time goes:
time: 331 us; the launch traced here: 329 us
  waiting for transfers between devices  143 us (43%)
  blocking collectives  54.6 us (16%)
  matrix products  40.6 us (12%)
  local copies, waits for them, and re-layouts  39.8 us (12%)
  starting transfers between devices  17.5 us (5%)
  between operations  17.1 us (5%)
  other arithmetic  16.6 us (5%)
    unnamed x2, waiting for transfers between devices  134 us
    psum x1, blocking collectives, body(): lax.psum((jnp.sum(advantages), jnp.sum(advantages * advantages)), ('team'...  42.2 us
    all_to_all x1, waiting for transfers between devices, body(): lax.all_to_all(input_grad.reshape(item_count, env_devs, per_peer, model_w...  9.11 us
    dot_general x6, matrix products, trans_times(): lax.dot_general(left_side, right_side, (((0,), (0,)), ((), ())), preferre...  8.25 us
    unnamed x43, local copies, waits for them, and re-layouts  7.7 us
    all_to_all x1, starting transfers between devices, body(): lax.all_to_all(outgoing_targets, 'env', split_axis=1, concat_axis=1, tile...  7.28 us
    dot_general x5, matrix products, times_trans(): lax.dot_general(left_side, right_side, (((1,), (1,)), ((), ())), preferre...  6.74 us
    psum x1, blocking collectives, body(): team_sums = lax.psum(trans_times(team_low, features), 'team')  6.68 us
  transfers between devices with their start and end apart: 4, of which 2 were waited for; matrix products, arithmetic and copies ran while one was open for 5% of the time, Pallas kernels for 0%

commit v1 on v0

v1 whole, which is shorter than its diff:
```python
import functools
import math

import jax
import jax.numpy as jnp
from jax import lax
from jax.experimental import pallas as pl
from jax.experimental.pallas import tpu as pltpu
from jax.sharding import PartitionSpec as P

HEADS = 4
TEAMS = 4
ENV_AGENTS = 256
ENV_DEV = 2


KL_WEIGHT = 0.5
NORM_EPS = 1e-05


def matmul(left_side, right_side):
    return jnp.dot(left_side, right_side, preferred_element_type=jnp.float32)


def times_trans(left_side, right_side):
    return lax.dot_general(
        left_side, right_side, (((1,), (1,)), ((), ())), preferred_element_type=jnp.float32
    )


def trans_times(left_side, right_side):
    return lax.dot_general(
        left_side, right_side, (((0,), (0,)), ((), ())), preferred_element_type=jnp.float32
    )


def normalize(values):
    center = values - jnp.mean(values, axis=-1, keepdims=True)
    spread = jnp.sqrt(jnp.mean(center * center, axis=-1, keepdims=True) + NORM_EPS)
    return (center / spread, spread)


def normalize_back(gradient, normed, spread):
    mean_grad = jnp.mean(gradient, axis=-1, keepdims=True)
    mean_along = jnp.mean(gradient * normed, axis=-1, keepdims=True)
    return (gradient - mean_grad - normed * mean_along) / spread


def critic_math(rows_of, targets_of, gain, w_query, w_key, w_value, grad_to, wgrad_ref):
    width = w_query.shape[0]
    head_width = width // HEADS
    factor = 1.0 / math.sqrt(head_width)
    totals = [None, None]
    for item in range(ENV_DEV):
        rows_in = rows_of(item).astype(jnp.float32)
        input_hat, input_spread = normalize(rows_in)
        normed = (input_hat * gain).astype(jnp.bfloat16)
        query = matmul(normed, w_query).astype(jnp.bfloat16)
        keys = matmul(normed, w_key).astype(jnp.bfloat16)
        cols = [slice(h * head_width, (h + 1) * head_width) for h in range(HEADS)]
        attention = []
        attended = []
        for c in cols:
            raised = jnp.exp(times_trans(query[:, c], keys[:, c]) * factor)
            attn = raised / jnp.sum(raised, axis=-1, keepdims=True)
            attention.append(attn)
            attended.append(matmul(attn.astype(jnp.bfloat16), normed[:, c]))
        mixed = rows_in + jnp.concatenate(attended, axis=1)
        mixed_hat, mixed_spread = normalize(mixed)
        value_out = jnp.sum(mixed_hat * w_value, axis=-1, keepdims=True)
        value_grad = value_out - targets_of(item)
        mixed_grad = normalize_back(value_grad * w_value, mixed_hat, mixed_spread)
        out_grad = mixed_grad.astype(jnp.bfloat16)
        query_grads = []
        key_grads = []
        sides = []
        for h, c in enumerate(cols):
            attn = attention[h]
            prob_grad = times_trans(out_grad[:, c], normed[:, c])
            sides.append(trans_times(attn.astype(jnp.bfloat16), out_grad[:, c]))
            along = jnp.sum(attn * prob_grad, axis=-1, keepdims=True)
            score_low = (attn * (prob_grad - along) * factor).astype(jnp.bfloat16)
            query_grads.append(matmul(score_low, keys[:, c]).astype(jnp.bfloat16))
            key_grads.append(trans_times(score_low, query[:, c]).astype(jnp.bfloat16))
        query_grad = jnp.concatenate(query_grads, axis=1)
        key_grad = jnp.concatenate(key_grads, axis=1)
        normed_grad = (
            times_trans(query_grad, w_query)
            + times_trans(key_grad, w_key)
            + jnp.concatenate(sides, axis=1)
        )
        back = mixed_grad + normalize_back(normed_grad * gain, input_hat, input_spread)
        grad_to(item, back.astype(jnp.bfloat16))
        for i, grad in enumerate((query_grad, key_grad)):
            part = trans_times(normed, grad)
            totals[i] = part if item == 0 else totals[i] + part
    for i in range(2):
        wgrad_ref[:, i * width : (i + 1) * width] = totals[i].astype(wgrad_ref.dtype)


def critic_kernel(rows_ref, tail_ref, gain_ref, wq_ref, wk_ref, wv_ref, grad_ref, wgrad_ref):
    peers = rows_ref.shape[0]
    width = rows_ref.shape[2]
    per_peer = ENV_AGENTS // peers

    def rows_of(item):
        part = rows_ref[:, item * per_peer : (item + 1) * per_peer, :].astype(jnp.float32)
        return part.reshape(ENV_AGENTS, width)

    def targets_of(item):
        row_id = lax.broadcasted_iota(jnp.int32, (ENV_AGENTS, peers), 0)
        peer_id = lax.broadcasted_iota(jnp.int32, (ENV_AGENTS, peers), 1)
        pick = (row_id // per_peer == peer_id).astype(jnp.bfloat16)
        spread = matmul(pick, tail_ref[:, 0:128])
        row_id = lax.broadcasted_iota(jnp.int32, (ENV_AGENTS, 128), 0)
        lane = lax.broadcasted_iota(jnp.int32, (ENV_AGENTS, 128), 1)
        keep = lane == row_id % per_peer + item * per_peer
        return jnp.sum(jnp.where(keep, spread, 0.0), axis=1, keepdims=True)

    def grad_to(item, value):
        value = value.astype(jnp.float32).reshape(peers, per_peer, width)
        grad_ref[:, item * per_peer : (item + 1) * per_peer, :] = value.astype(jnp.bfloat16)

    critic_math(
        rows_of,
        targets_of,
        gain_ref[...],
        wq_ref[...],
        wk_ref[...],
        wv_ref[...],
        grad_to,
        wgrad_ref,
    )


def critic_call(rows, tail, norm_gain, w_query, w_key, w_value):
    peers = rows.shape[0]
    width = rows.shape[2]
    per_device = ENV_DEV * ENV_AGENTS // peers
    return pl.pallas_call(
        critic_kernel,
        out_shape=(
            jax.ShapeDtypeStruct((peers, per_device, width), jnp.bfloat16),
            jax.ShapeDtypeStruct((width, 2 * width), jnp.bfloat16),
        ),
        in_specs=[pl.BlockSpec(memory_space=pltpu.VMEM)] * 6,
        out_specs=(pl.BlockSpec(memory_space=pltpu.VMEM),) * 2,
        compiler_params=pltpu.CompilerParams(vmem_limit_bytes=48 * 1024 * 1024),
        cost_estimate=pl.CostEstimate(
            flops=6_000_000_000, bytes_accessed=4_000_000, transcendentals=600_000
        ),
    )(rows, tail, norm_gain[None, :], w_query, w_key, w_value[None, :])


def log2(count):
    return count.bit_length() - 1


def scatter_kernel(team_bits, env_bits, orders, *refs):
    count = len(orders)
    stages = team_bits + env_bits
    ins, outs = refs[:count], refs[count : 2 * count]
    refs = refs[2 * count :]
    recv = [refs[i * stages : (i + 1) * stages] for i in range(count)]
    refs = refs[count * stages :]
    sums = [refs[i * (stages - 1) : (i + 1) * (stages - 1)] for i in range(count)]
    refs = refs[count * (stages - 1) :]
    send = [refs[i * (stages - 1) : (i + 1) * (stages - 1)] for i in range(count)]
    send_sem, recv_sem = refs[count * (stages - 1) :]
    team, env = lax.axis_index("team"), lax.axis_index("env")

    def place(bit):
        if bit < team_bits:
            step = 1 << (team_bits - 1 - bit)
            mine = (team // step) % 2
            return mine, (team + (1 - 2 * mine) * step, env)
        step = 1 << (stages - 1 - bit)
        mine = (env // step) % 2
        return mine, (team, env + (1 - 2 * mine) * step)

    places = [place(bit) for bit in range(stages)]
    barrier = pltpu.get_barrier_semaphore()
    for _, peer in places:
        pl.semaphore_signal(barrier, inc=1, device_id=peer, device_id_type=pl.DeviceIdType.MESH)
    pl.semaphore_wait(barrier, stages)

    def start(i, stage):
        bit = orders[i][stage]
        axis = sum(1 for b in range(bit) if b not in orders[i][:stage])
        mine, peer = places[bit]
        before = (slice(None),) * axis
        if stage == 0:
            source = ins[i].at[before + (1 - mine,)]
        else:
            source = send[i][stage - 1]
            source[...] = sums[i][stage - 1][before + (1 - mine,)].astype(jnp.bfloat16)
        copy = pltpu.make_async_remote_copy(
            src_ref=source,
            dst_ref=recv[i][stage],
            send_sem=send_sem.at[i, stage],
            recv_sem=recv_sem.at[i, stage],
            device_id=peer,
            device_id_type=pl.DeviceIdType.MESH,
        )
        copy.start()
        return copy, before + (mine,)

    flight = [start(i, 0) for i in range(count)]
    for stage in range(stages):
        for i in range(count):
            copy, kept = flight[i]
            copy.wait()
            held = ins[i] if stage == 0 else sums[i][stage - 1]
            total = held[kept].astype(jnp.float32) + recv[i][stage][...].astype(jnp.float32)
            if stage == stages - 1:
                outs[i][...] = total
            else:
                sums[i][stage][...] = total
                flight[i] = start(i, stage + 1)


def scatter_sums(parts, team_devs, env_devs):
    team_bits, env_bits = log2(team_devs), log2(env_devs)
    stages = team_bits + env_bits
    rows = parts[0].shape[0] // (team_devs * env_devs)
    team_order = list(range(team_bits))[::-1]
    env_order = list(range(team_bits, stages))[::-1]
    first = team_order + env_order
    second = team_order[:1] + env_order + team_order[1:]
    orders = [first, first, second, second][: len(parts)]

    def left(part, stage, dtype):
        return pltpu.VMEM((2,) * (stages - 1 - stage) + (rows, part.shape[1]), dtype)

    scratch = [left(p, s, jnp.bfloat16) for p in parts for s in range(stages)]
    scratch += [left(p, s, jnp.float32) for p in parts for s in range(stages - 1)]
    scratch += [left(p, s + 1, jnp.bfloat16) for p in parts for s in range(stages - 1)]
    scratch += [pltpu.SemaphoreType.DMA((len(parts), stages))] * 2
    return pl.pallas_call(
        functools.partial(scatter_kernel, team_bits, env_bits, orders),
        out_shape=tuple(jax.ShapeDtypeStruct((rows, p.shape[1]), jnp.float32) for p in parts),
        in_specs=[pl.BlockSpec(memory_space=pltpu.VMEM)] * len(parts),
        out_specs=(pl.BlockSpec(memory_space=pltpu.VMEM),) * len(parts),
        scratch_shapes=scratch,
        compiler_params=pltpu.CompilerParams(
            collective_id=0, has_side_effects=True, vmem_limit_bytes=40 * 1024 * 1024
        ),
        cost_estimate=pl.CostEstimate(flops=5_000_000, bytes_accessed=8_000_000, transcendentals=0),
    )(*[p.reshape((2,) * stages + (rows, p.shape[1])) for p in parts])


def split_three(value):
    high = lax.reduce_precision(value, 8, 7)
    rest = value - high
    middle = lax.reduce_precision(rest, 8, 7)
    low = lax.reduce_precision(rest - middle, 8, 7)
    return [high, middle, low]


def body(
    features,
    team_of,
    env_of,
    actions,
    old_logp,
    advantages,
    returns,
    w_hidden,
    w_comm,
    w_policy,
    norm_gain,
    w_query,
    w_key,
    w_value,
):
    agent_rows, model_width = features.shape
    policy_width = w_policy.shape[1]
    team_devs = lax.axis_size("team")
    env_devs = lax.axis_size("env")
    devices_all = team_devs * env_devs
    members = team_devs * agent_rows // TEAMS
    inv_peers = 1.0 / (members - 1)
    team_mask = team_of[:, None] == jnp.arange(TEAMS, dtype=jnp.int32)[None, :]
    team_low = team_mask.astype(jnp.bfloat16)
    team_full = team_mask.astype(jnp.float32)
    own_sums = jnp.stack([jnp.sum(advantages), jnp.sum(advantages * advantages)])
    own_sums = jnp.pad(own_sums, (0, model_width - 2))[None, :]
    first_sums = lax.psum(
        jnp.concatenate([trans_times(team_low, features), own_sums], axis=0), "team"
    )
    team_sums = first_sums[:TEAMS]
    team_share = jnp.dot(
        team_full, team_sums, precision=lax.Precision.HIGHEST, preferred_element_type=jnp.float32
    )
    message = ((team_share - features.astype(jnp.float32)) * inv_peers).astype(jnp.bfloat16)
    pre_act = matmul(features, w_hidden) + matmul(message, w_comm)
    hidden = jnp.tanh(pre_act).astype(jnp.bfloat16)
    logits = matmul(hidden, w_policy)
    raised = jnp.exp(logits)
    totals = jnp.sum(raised, axis=-1, keepdims=True)
    probs_all = raised / totals
    log_probs = logits - jnp.log(totals)
    chosen = (actions[:, None] == jnp.arange(policy_width, dtype=jnp.int32)[None, :]).astype(
        jnp.float32
    )
    log_chosen = jnp.sum(chosen * log_probs, axis=-1)
    per_peer = ENV_AGENTS // env_devs
    target_device = env_of // ENV_DEV % env_devs
    target_env = env_of % ENV_DEV
    key = target_device * ENV_DEV + target_env
    key_mask = (key[:, None] == jnp.arange(ENV_DEV * env_devs, dtype=jnp.int32)[None, :]).astype(
        jnp.bfloat16
    )
    counter = jnp.arange(agent_rows, dtype=jnp.int32)
    earlier = (counter[:, None] > counter[None, :]).astype(jnp.bfloat16)
    ranks = matmul(earlier, key_mask)
    rank = jnp.sum(ranks * key_mask.astype(jnp.float32), axis=-1).astype(jnp.int32)
    slot = key * per_peer + rank
    placing = (slot[None, :] == counter[:, None]).astype(jnp.bfloat16)
    per_device = ENV_DEV * per_peer
    outgoing = matmul(placing, hidden).astype(jnp.bfloat16)
    outgoing_targets = matmul(placing, returns[:, None]).astype(jnp.bfloat16)
    outgoing_targets = outgoing_targets.reshape(env_devs, per_device)
    pieces = split_three(first_sums[TEAMS, 0]) + split_three(first_sums[TEAMS, 1])
    sent_sums = jnp.broadcast_to(jnp.stack(pieces).astype(jnp.bfloat16)[None, :], (env_devs, 6))
    tail = jnp.concatenate([outgoing_targets, sent_sums], axis=1)
    tail = jnp.pad(tail, ((0, 0), (0, model_width - tail.shape[1])))
    tail = jnp.pad(tail[:, None, :], ((0, 0), (0, 15), (0, 0)))
    arriving = lax.all_to_all(
        jnp.concatenate([outgoing.reshape(env_devs, per_device, model_width), tail], axis=1),
        "env",
        split_axis=0,
        concat_axis=0,
        tiled=True,
    )
    arrived_tail = arriving[:, per_device, :]
    arrived_sums = jnp.sum(
        arrived_tail[:, per_device : per_device + 6].astype(jnp.float32), axis=0
    )
    advantage_total = jnp.sum(arrived_sums[:3])
    advantage_squares = jnp.sum(arrived_sums[3:])
    agent_total = agent_rows * devices_all
    advantage_mean = advantage_total / agent_total
    advantage_spread = advantage_squares / agent_total - advantage_mean * advantage_mean
    scaled_advantage = (advantages - advantage_mean) / jnp.sqrt(advantage_spread + NORM_EPS)
    ratios = jnp.exp(log_chosen - old_logp)
    delta_grad = -ratios * scaled_advantage + KL_WEIGHT * (ratios - 1.0)
    logit_grad = (delta_grad[:, None] * (chosen - probs_all)).astype(jnp.bfloat16)
    input_grad, critic_parts = critic_call(
        arriving, arrived_tail, norm_gain, w_query, w_key, w_value
    )
    returned = lax.all_to_all(input_grad, "env", split_axis=0, concat_axis=0, tiled=True)
    critic_grad = trans_times(placing, returned.reshape(agent_rows, model_width))
    hidden_grad = times_trans(logit_grad, w_policy) + critic_grad
    hidden_full = hidden.astype(jnp.float32)
    pre_grad = (hidden_grad * (1.0 - hidden_full * hidden_full)).astype(jnp.bfloat16)
    message_grad = times_trans(pre_grad, w_comm)
    local_message = lax.dot_general(
        team_full,
        message_grad,
        (((0,), (0,)), ((), ())),
        precision=lax.Precision.HIGHEST,
        preferred_element_type=jnp.float32,
    )
    message_sums = lax.psum(local_message, "team")
    message_share = jnp.dot(
        team_full, message_sums, precision=lax.Precision.HIGHEST, preferred_element_type=jnp.float32
    )
    grad_input = (
        times_trans(pre_grad, w_hidden) + (message_share - message_grad) * inv_peers
    ).astype(jnp.bfloat16)
    parts = [
        trans_times(features, pre_grad).astype(jnp.bfloat16),
        trans_times(message, pre_grad).astype(jnp.bfloat16),
        trans_times(hidden, logit_grad).astype(jnp.bfloat16),
        critic_parts,
    ]
    if model_width // devices_all % 16 == 0:
        summed = scatter_sums(parts, team_devs, env_devs)
    else:
        summed = [
            lax.psum_scatter(
                p.astype(jnp.float32), ("team", "env"), scatter_dimension=0, tiled=True
            )
            for p in parts
        ]
    grad_w_hidden, grad_w_comm, grad_w_policy, critic_sums = summed
    grad_w_query = critic_sums[:, :model_width]
    grad_w_key = critic_sums[:, model_width:]
    return (grad_input, grad_w_hidden, grad_w_comm, grad_w_policy, grad_w_query, grad_w_key)


def solution(mesh):
    in_specs = (
        P(("team", "env"), None),
        P(("team", "env")),
        P(("team", "env")),
        P(("team", "env")),
        P(("team", "env")),
        P(("team", "env")),
        P(("team", "env")),
        P(),
        P(),
        P(),
        P(),
        P(),
        P(),
        P(),
    )
    out_specs = (
        P(("team", "env"), None),
        P(("team", "env"), None),
        P(("team", "env"), None),
        P(("team", "env"), None),
        P(("team", "env"), None),
        P(("team", "env"), None),
    )
    return jax.shard_map(body, mesh=mesh, in_specs=in_specs, out_specs=out_specs, check_vma=False)
```

time: 331 us -> 123 us (0.37)
  waiting for transfers between devices: 143 us -> 22.6 us
  blocking collectives: 54.6 us -> 18.5 us
  local copies, waits for them, and re-layouts: 39.8 us -> 5.75 us
  Pallas kernels: 0 us -> 32.2 us
  matrix products: 40.6 us -> 12.8 us
  other arithmetic: 16.6 us -> 5.09 us
  starting transfers between devices: 17.5 us -> 10.4 us
    unnamed x2 -> x0, waiting for transfers between devices: 134 us -> none
    psum x2 -> x1, blocking collectives: 48.9 us -> 12.7 us  [body(): lax.psum(jnp.concatenate([trans_times(team_low, features), own_sums], axi...]
    pallas_call x0 -> x2, Pallas kernels: none -> 32.2 us  [the longest x1 25.3 us: scatter_sums(): pl.pallas_call(functools.partial(scatter_kernel, team_bits, env_bits, ord...]
    dot_general x6 -> x0, matrix products: 19.7 us -> none  [the longest x1 5.56 us: critic_pass(): jnp.einsum('chqk,cqhd->ckhd', score_low, query_heads, preferred_element_t...]
    all_to_all x3 -> x2, waiting for transfers between devices: 9.12 us -> 22.6 us  [the longest x1 14.8 us: body(): lax.all_to_all(jnp.concatenate([outgoing.reshape(env_devs, per_device, mo...]
    reshape x8 -> x1, local copies, waits for them, and re-layouts: 8.34 us -> 0.09 us  [body(): outgoing_targets = outgoing_targets.reshape(env_devs, per_device)]
    gather x3 -> x0, local copies, waits for them, and re-layouts: 7.58 us -> none  [the longest x1 3.64 us: body(): outgoing_targets = returns[ordering].reshape(ENV_DEV, env_devs, per_peer)]
    sort x2 -> x0, other arithmetic: 7.54 us -> none  [the longest x1 3.77 us: body(): inverse = jnp.argsort(ordering, stable=True)]
  transfers between devices with their start and end apart: 4 -> 2, of which waited for: 2 -> 2; matrix products, arithmetic and copies ran while one was open for 5% -> 3% of each run, Pallas kernels for 0% -> 0%
where the time goes in v1:
time: 123 us; the launch traced here: 122 us
  Pallas kernels  32.2 us (26%)
  waiting for transfers between devices  22.6 us (18%)
  blocking collectives  18.5 us (15%)
  between operations  14.7 us (12%)
  matrix products  12.8 us (10%)
  starting transfers between devices  10.4 us (8%)
  local copies, waits for them, and re-layouts  5.75 us (5%)
  other arithmetic  5.09 us (4%)
    pallas_call x1, Pallas kernels, scatter_sums(): pl.pallas_call(functools.partial(scatter_kernel, team_bits, env_bits, ord...  25.3 us
    all_to_all x1, waiting for transfers between devices, body(): lax.all_to_all(jnp.concatenate([outgoing.reshape(env_devs, per_device, mo...  14.8 us
    psum x1, blocking collectives, body(): lax.psum(jnp.concatenate([trans_times(team_low, features), own_sums], axi...  12.7 us
    all_to_all x1, waiting for transfers between devices, body(): lax.all_to_all(input_grad, 'env', split_axis=0, concat_axis=0, tiled=True)  7.83 us
    pallas_call x1, Pallas kernels, critic_call(): pl.pallas_call(critic_kernel, out_shape=(jax.ShapeDtypeStruct((peers, per...  6.96 us
    all_to_all x1, starting transfers between devices, body(): lax.all_to_all(jnp.concatenate([outgoing.reshape(env_devs, per_device, mo...  5.97 us
    psum x1, blocking collectives, body(): message_sums = lax.psum(local_message, 'team')  5.8 us
    dot_general x5, matrix products, trans_times(): lax.dot_general(left_side, right_side, (((0,), (0,)), ((), ())), preferre...  4.7 us
  transfers between devices with their start and end apart: 2, of which 2 were waited for; matrix products, arithmetic and copies ran while one was open for 3% of the time, Pallas kernels for 0%

profile of v1, /device:TPU:0, one launch (start us, length us, event | category | flops | bytes accessed | tf_op | source)
XLA Modules:
  0.0 122.1 jit_solution(15704099587342822835)
XLA Ops:
  0.7 1.3 %fusion.30 = (f32[]{:T(128)}, f32[]{:T(128)}) fusion(f32[512]{0:T(512)} %param.19), kind=kLoop, calls=%fused_computation.70 | loop fusion | flops 1534 | bytes 2056 | tf_op jit(solution)/shard_map/reduce_sum | solution.py:286
  2.0 1.4 %select_maximum_fusion = f32[512]{0:T(512)S(1)} fusion(f32[1]{0:T(128)} %bitcast.1, f32[1]{0:T(128)} %bitcast), kind=kLoop, calls=%fused_computation.60 | loop fusion | flops 2048 | bytes 2056 | tf_op jit(solution)/shard_map/stack | solution.py:286
  3.4 1.4 %fusion.16 = f32[4,512]{1,0:T(4,128)S(1)} fusion(bf16[512,512]{1,0:T(8,128)(2,1)} %param.14, s32[512]{0:T(512)} %param.15), kind=kOutput, calls=%fused_computation.32 | convolution fusion | flops 2099200 | bytes 534528 | tf_op jit(solution)/shard_map/dot_general | solution.py:32
  4.8 12.7 %psum.14 = f32[5,512]{1,0:T(8,128)S(1)} all-reduce(f32[5,512]{1,0:T(8,128)S(1)} %pad_maximum_fusion), channel_id=1, replica_groups=mesh['team'=4,'env'=8] {'team'}, use_global_device_ids=true, to_apply=%region_2.3 | all-reduce | flops 2560 | bytes 20480 | tf_op jit(solution)/shard_map/psum | solution.py:288
  27.9 1.7 %fusion.6 = bf16[512,512]{1,0:T(8,128)(2,1)S(1)} fusion(bf16[512,512]{1,0:T(8,128)(2,1)} %param.14, s32[512]{0:T(512)} %param.15, f32[5,512]{1,0:T(8,128)S(1)} %psum.14), kind=kOutput, calls=%fused_computation.15 | convolution fusion | flops 13633536 | bytes 1058816 | tf_op jit(solution)/shard_map/dot_general | solution.py:292
  31.5 1.4 %stack.39 = bf16[6]{0:T(256)(128)(2,1)S(1)} concatenate(bf16[1]{0:T(256)(128)(2,1)} %bitcast.6, bf16[1]{0:T(256)(128)(2,1)} %bitcast.7, bf16[1]{0:T(256)(128)(2,1)} %bitcast.8, bf16[1]{0:T(256)(128)(2,1)} %bitcast.10, bf16[1]{0:T(256)(128)(2,1)} %bitcast.11, bf16[1]{0:T(256)(128)(2,1)} %bitcast.12), dimensions={0} | concatenate | bytes 24 | tf_op jit(solution)/shard_map/stack | solution.py:325
  34.5 0.9 fusion.11
  35.4 6.0 %all-to-all-start = ((bf16[8,80,512]{2,1,0:T(8,128)(2,1)}), bf16[8,80,512]{2,1,0:T(8,128)(2,1)S(1)}, u32[]{:S(2)}, u32[]{:S(2)}) async-start(bf16[8,80,512]{2,1,0:T(8,128)(2,1)} %fusion.11), calls=%async_computation | async-start | bytes 1310720 | tf_op jit(solution)/shard_map/all_to_all | solution.py:329
  41.7 0.6 select_reduce_fusion
  42.4 14.8 %all-to-all-done.rows_ref = bf16[8,80,512]{2,1,0:T(8,128)(2,1)S(1)} async-done(((bf16[8,80,512]{2,1,0:T(8,128)(2,1)}), bf16[8,80,512]{2,1,0:T(8,128)(2,1)S(1)}, u32[]{:S(2)}, u32[]{:S(2)}) %all-to-all-start) | async-done | bytes 655392 | tf_op jit(solution)/shard_map/all_to_all | solution.py:329
  57.2 7.0 %shard_map.181 = (bf16[8,64,512]{2,1,0:T(8,128)(2,1)}, bf16[512,1024]{1,0:T(8,128)(2,1)S(1)}) custom-call(bf16[8,80,512]{2,1,0:T(8,128)(2,1)S(1)} %all-to-all-done.rows_ref, bf16[8,512]{1,0:T(8,128)(2,1)S(1)} %bitcast.53, f32[1,512]{1,0:T(1,128)S(1)} %bitcast.55, bf16[512,512]{1,0:T(8,128)(2,1)S(1)} %copy-done.1, bf16[512,512]{1,0:T(8,128)(2,1)S(1)} %copy-done.2, ...), custom_call_target="tpu_custom_call" | custom-call | flops 6000000000 | bytes 4000000 | tf_op jit(solution)/shard_map/pallas_call | solution.py:140
  64.2 4.5 %all-to-all-start.1 = ((bf16[8,64,512]{2,1,0:T(8,128)(2,1)}), bf16[8,64,512]{2,1,0:T(8,128)(2,1)}, u32[]{:S(2)}, u32[]{:S(2)}) async-start(bf16[8,64,512]{2,1,0:T(8,128)(2,1)} %get-tuple-element.12), calls=%async_computation.1 | async-start | bytes 1048576 | tf_op jit(solution)/shard_map/all_to_all | solution.py:352
  68.8 0.7 slice_reduce_fusion.1
  72.6 1.3 %fusion.29 = f32[512,512]{1,0:T(8,128)} fusion(bf16[512,128]{1,0:T(8,128)(2,1)S(1)} %copy-done.14, f32[512,128]{0,1:T(8,128)S(1)} %get-tuple-element.27, f32[512]{0:T(512)S(1)} %copy-done.17, f32[512]{0:T(512)S(1)} %fusion.24, s32[512]{0:T(512)S(1)} %copy-done.19), kind=kOutput, calls=%fused_computation.69 | convolution fusion | flops 67502080 | bytes 1447936 | tf_op jit(solution)/shard_map/dot_general | solution.py:26
  73.9 7.8 %all-to-all-done.1 = bf16[8,64,512]{2,1,0:T(8,128)(2,1)} async-done(((bf16[8,64,512]{2,1,0:T(8,128)(2,1)}), bf16[8,64,512]{2,1,0:T(8,128)(2,1)}, u32[]{:S(2)}, u32[]{:S(2)}) %all-to-all-start.1) | async-done | bytes 524320 | tf_op jit(solution)/shard_map/all_to_all | solution.py:352
  81.8 2.0 %fusion.5 = bf16[512,512]{1,0:T(8,128)(2,1)S(1)} fusion(f32[512,512]{1,0:T(8,128)} %fusion.29, bf16[512,512]{1,0:T(8,128)(2,1)} %bitcast.17, bf16[512,512]{1,0:T(8,128)(2,1)S(1)} %copy-done.8, s32[512]{0:T(512)S(1)} %copy-done.24), kind=kOutput, calls=%fused_computation.11 | convolution fusion | flops 270270464 | bytes 2623488 | tf_op jit(solution)/shard_map/dot_general | solution.py:32
  85.7 25.3 %shard_map.182 = (f32[16,512]{1,0:T(8,128)S(1)}, f32[16,512]{1,0:T(8,128)S(1)}, f32[16,128]{1,0:T(8,128)S(1)}, f32[16,1024]{1,0:T(8,128)S(1)}) custom-call(bf16[2,2,2,2,2,16,512]{6,5,4,3,2,1,0:T(8,128)(2,1)S(1)} %bitcast.49, bf16[2,2,2,2,2,16,512]{6,5,4,3,2,1,0:T(8,128)(2,1)S(1)} %bitcast.51, bf16[2,2,2,2,2,16,128]{6,5,4,3,2,1,0:T(8,128)(2,1)S(1)} %bitcast.52, ...), custom_call_target="tpu_custom_call" | custom-call | flops 5000000 | bytes 8000000 | tf_op jit(solution)/shard_map/pallas_call | solution.py:239
  111.0 0.6 fusion.31
  112.2 5.8 %psum.15 = f32[4,512]{1,0:T(4,128)S(1)} all-reduce(f32[4,512]{1,0:T(4,128)S(1)} %fusion.15), channel_id=1, replica_groups=mesh['team'=4,'env'=8] {'team'}, use_global_device_ids=true, to_apply=%region_9.10 | all-reduce | flops 2048 | bytes 16384 | tf_op jit(solution)/shard_map/psum | solution.py:365
  118.0 0.7 fusion
  119.0 1.3 %fusion.8 = bf16[512,512]{1,0:T(8,128)(2,1)} fusion(f32[512,512]{1,0:T(8,128)S(1)} %fusion, bf16[512,512]{1,0:T(8,128)(2,1)S(1)} %fusion.5, bf16[512,512]{1,0:T(8,128)(2,1)S(1)} %copy-done.12), kind=kOutput, calls=%fused_computation.17 | convolution fusion | flops 268959744 | bytes 2621440 | tf_op jit(solution)/shard_map/dot_general | solution.py:26
  120.3 0.6 copy.32
  120.9 0.6 copy.33
  121.5 0.6 copy.34
  (81 shorter events, 6.5 us)
Async XLA Ops:
  0.6 32.9 %copy-start = (bf16[512,512]{1,0:T(8,128)(2,1)S(1)}, bf16[512,512]{1,0:T(8,128)(2,1)}, u32[]{:S(2)}) copy-start(bf16[512,512]{1,0:T(8,128)(2,1)} %param.22) | copy-start | bytes 1572868
  0.6 30.1 %copy-start.21 = (s32[512]{0:T(512)S(1)}, s32[512]{0:T(512)}, u32[]{:S(2)}) copy-start(s32[512]{0:T(512)} %param.16) | copy-start | bytes 6148
  0.7 30.4 %copy-start.26 = (bf16[512]{0:T(512)(128)(2,1)S(1)}, bf16[512]{0:T(512)(128)(2,1)}, u32[]{:S(2)}) copy-start(bf16[512]{0:T(512)(128)(2,1)} %param.20) | copy-start | bytes 3076
  3.4 29.7 %copy-start.5 = (bf16[512,512]{1,0:T(8,128)(2,1)S(1)}, bf16[512,512]{1,0:T(8,128)(2,1)}, u32[]{:S(2)}) copy-start(bf16[512,512]{1,0:T(8,128)(2,1)} %param.14) | copy-start | bytes 1572868
  3.4 29.7 %copy-start.11 = (bf16[512,512]{1,0:T(8,128)(2,1)S(1)}, bf16[512,512]{1,0:T(8,128)(2,1)}, u32[]{:S(2)}) copy-start(bf16[512,512]{1,0:T(8,128)(2,1)} %param.21) | copy-start | bytes 1572868
  29.6 3.9 %copy-start.9 = (bf16[512,512]{1,0:T(8,128)(2,1)}, bf16[512,512]{1,0:T(8,128)(2,1)S(1)}, u32[]{:S(2)}) copy-start(bf16[512,512]{1,0:T(8,128)(2,1)S(1)} %fusion.6) | copy-start | bytes 1572868
  34.0 7.4 %copy-start.7 = (bf16[512,512]{1,0:T(8,128)(2,1)}, bf16[512,512]{1,0:T(8,128)(2,1)S(1)}, u32[]{:S(2)}) copy-start(bf16[512,512]{1,0:T(8,128)(2,1)S(1)} %fusion.7) | copy-start | bytes 1572868
  34.4 6.9 %copy-start.13 = (bf16[512,128]{1,0:T(8,128)(2,1)S(1)}, bf16[512,128]{1,0:T(8,128)(2,1)}, u32[]{:S(2)}) copy-start(bf16[512,128]{1,0:T(8,128)(2,1)} %param.23) | copy-start | bytes 393220
  35.4 6.4 %copy-start.18 = (s32[512]{0:T(512)S(1)}, s32[512]{0:T(512)}, u32[]{:S(2)}) copy-start(s32[512]{0:T(512)} %param.17) | copy-start | bytes 6148
  35.4 21.8 %copy-start.1 = (bf16[512,512]{1,0:T(8,128)(2,1)S(1)}, bf16[512,512]{1,0:T(8,128)(2,1)}, u32[]{:S(2)}) copy-start(bf16[512,512]{1,0:T(8,128)(2,1)} %wq_ref.1) | copy-start | bytes 1572868
  35.4 21.9 %copy-start.2 = (bf16[512,512]{1,0:T(8,128)(2,1)S(1)}, bf16[512,512]{1,0:T(8,128)(2,1)}, u32[]{:S(2)}) copy-start(bf16[512,512]{1,0:T(8,128)(2,1)} %wk_ref.1) | copy-start | bytes 1572868
  35.4 21.9 %copy-start.3 = (f32[512]{0:T(512)S(1)}, f32[512]{0:T(512)}, u32[]{:S(2)}) copy-start(f32[512]{0:T(512)} %param.24) | copy-start | bytes 6148
  35.4 21.9 %copy-start.4 = (f32[512]{0:T(512)S(1)}, f32[512]{0:T(512)}, u32[]{:S(2)}) copy-start(f32[512]{0:T(512)} %param.27) | copy-start | bytes 6148
  35.4 21.8 %all-to-all-start = ((bf16[8,80,512]{2,1,0:T(8,128)(2,1)}), bf16[8,80,512]{2,1,0:T(8,128)(2,1)S(1)}, u32[]{:S(2)}, u32[]{:S(2)}) async-start(bf16[8,80,512]{2,1,0:T(8,128)(2,1)} %fusion.11), calls=%async_computation | async-start | bytes 1310720 | tf_op jit(solution)/shard_map/all_to_all | solution.py:329
  41.7 15.5 %copy-start.16 = (f32[512]{0:T(512)}, f32[512]{0:T(512)S(1)}, u32[]{:S(2)}) copy-start(f32[512]{0:T(512)S(1)} %get-tuple-element.26) | copy-start | bytes 6148
  64.2 7.9 %copy-start.20 = (f32[512]{0:T(512)S(1)}, f32[512]{0:T(512)}, u32[]{:S(2)}) copy-start(f32[512]{0:T(512)} %select_reduce_fusion) | copy-start | bytes 6148
  64.2 7.9 %copy-start.22 = (f32[512]{0:T(512)S(1)}, f32[512]{0:T(512)}, u32[]{:S(2)}) copy-start(f32[512]{0:T(512)} %param.19) | copy-start | bytes 6148
  64.2 7.9 %copy-start.25 = (f32[512]{0:T(512)S(1)}, f32[512]{0:T(512)}, u32[]{:S(2)}) copy-start(f32[512]{0:T(512)} %param.18) | copy-start | bytes 6148
  64.2 8.0 %copy-start.8 = (bf16[512,512]{1,0:T(8,128)(2,1)S(1)}, bf16[512,512]{1,0:T(8,128)(2,1)}, u32[]{:S(2)}) copy-start(bf16[512,512]{1,0:T(8,128)(2,1)} %copy-done.7) | copy-start | bytes 1572868
  64.2 8.0 %copy-start.17 = (f32[512]{0:T(512)S(1)}, f32[512]{0:T(512)}, u32[]{:S(2)}) copy-start(f32[512]{0:T(512)} %copy-done.16) | copy-start | bytes 6148
  64.2 8.0 %copy-start.19 = (s32[512]{0:T(512)S(1)}, s32[512]{0:T(512)}, u32[]{:S(2)}) copy-start(s32[512]{0:T(512)} %param.17) | copy-start | bytes 6148
  64.2 17.5 %all-to-all-start.1 = ((bf16[8,64,512]{2,1,0:T(8,128)(2,1)}), bf16[8,64,512]{2,1,0:T(8,128)(2,1)}, u32[]{:S(2)}, u32[]{:S(2)}) async-start(bf16[8,64,512]{2,1,0:T(8,128)(2,1)} %get-tuple-element.12), calls=%async_computation.1 | async-start | bytes 1048576 | tf_op jit(solution)/shard_map/all_to_all | solution.py:352
  72.6 9.2 %copy-start.24 = (s32[512]{0:T(512)S(1)}, s32[512]{0:T(512)}, u32[]{:S(2)}) copy-start(s32[512]{0:T(512)} %copy-done.23) | copy-start | bytes 6148
  85.7 25.9 %copy-start.15 = (s32[512]{0:T(512)S(1)}, s32[512]{0:T(512)}, u32[]{:S(2)}) copy-start(s32[512]{0:T(512)} %param.15) | copy-start | bytes 6148
  (5 other events, 10.8 us)

commit v2 on v0

v2 whole, which is shorter than its diff:
```python
import functools
import math

import jax
import jax.numpy as jnp
from jax import lax
from jax.experimental import pallas as pl
from jax.experimental.pallas import tpu as pltpu
from jax.sharding import PartitionSpec as P

HEADS = 4
TEAMS = 4
ENV_AGENTS = 256
ENV_DEV = 2


KL_WEIGHT = 0.5
NORM_EPS = 1e-05


def matmul(left_side, right_side):
    return jnp.dot(left_side, right_side, preferred_element_type=jnp.float32)


def times_trans(left_side, right_side):
    return lax.dot_general(
        left_side, right_side, (((1,), (1,)), ((), ())), preferred_element_type=jnp.float32
    )


def trans_times(left_side, right_side):
    return lax.dot_general(
        left_side, right_side, (((0,), (0,)), ((), ())), preferred_element_type=jnp.float32
    )


def normalize(values):
    center = values - jnp.mean(values, axis=-1, keepdims=True)
    spread = jnp.sqrt(jnp.mean(center * center, axis=-1, keepdims=True) + NORM_EPS)
    return (center / spread, spread)


def normalize_back(gradient, normed, spread):
    mean_grad = jnp.mean(gradient, axis=-1, keepdims=True)
    mean_along = jnp.mean(gradient * normed, axis=-1, keepdims=True)
    return (gradient - mean_grad - normed * mean_along) / spread


def log2(count):
    return count.bit_length() - 1


def critic_item(rows_in, targets, gain, w_query, w_key, w_value):
    width = w_query.shape[0]
    head_width = width // HEADS
    factor = 1.0 / math.sqrt(head_width)
    input_hat, input_spread = normalize(rows_in)
    normed = (input_hat * gain).astype(jnp.bfloat16)
    query = matmul(normed, w_query).astype(jnp.bfloat16)
    keys = matmul(normed, w_key).astype(jnp.bfloat16)
    cols = [slice(h * head_width, (h + 1) * head_width) for h in range(HEADS)]
    attention = []
    attended = []
    for c in cols:
        raised = jnp.exp(times_trans(query[:, c], keys[:, c]) * factor)
        attn = raised / jnp.sum(raised, axis=-1, keepdims=True)
        attention.append(attn)
        attended.append(matmul(attn.astype(jnp.bfloat16), normed[:, c]))
    mixed = rows_in + jnp.concatenate(attended, axis=1)
    mixed_hat, mixed_spread = normalize(mixed)
    value_out = jnp.sum(mixed_hat * w_value, axis=-1, keepdims=True)
    value_grad = value_out - targets
    mixed_grad = normalize_back(value_grad * w_value, mixed_hat, mixed_spread)
    out_grad = mixed_grad.astype(jnp.bfloat16)
    query_grads = []
    key_grads = []
    sides = []
    for h, c in enumerate(cols):
        attn = attention[h]
        prob_grad = times_trans(out_grad[:, c], normed[:, c])
        sides.append(trans_times(attn.astype(jnp.bfloat16), out_grad[:, c]))
        along = jnp.sum(attn * prob_grad, axis=-1, keepdims=True)
        score_low = (attn * (prob_grad - along) * factor).astype(jnp.bfloat16)
        query_grads.append(matmul(score_low, keys[:, c]).astype(jnp.bfloat16))
        key_grads.append(trans_times(score_low, query[:, c]).astype(jnp.bfloat16))
    query_grad = jnp.concatenate(query_grads, axis=1)
    key_grad = jnp.concatenate(key_grads, axis=1)
    normed_grad = (
        times_trans(query_grad, w_query)
        + times_trans(key_grad, w_key)
        + jnp.concatenate(sides, axis=1)
    )
    back = mixed_grad + normalize_back(normed_grad * gain, input_hat, input_spread)
    return back.astype(jnp.bfloat16), normed, query_grad, key_grad


def window_kernel(team_devs, env_devs, orders, scatter, *refs):
    team_bits, env_bits = log2(team_devs), log2(env_devs)
    stages = team_bits + env_bits
    (feat_ref, lane_ref, col_ref, wh_ref, wc_ref, wp_ref, gain_ref, wq_ref, wk_ref, wv_ref) = refs[:10]
    out_ref, outs = refs[10], refs[11:15]
    refs = refs[15:]
    (team_send, team_recv, msg_send, msg_recv, rows_send, rows_recv) = refs[:6]
    (tail_send, tail_recv, back_send, back_recv) = refs[6:10]
    (team_ss, team_rs, msg_ss, msg_rs, rows_ss, rows_rs) = refs[10:16]
    (tail_ss, tail_rs, back_ss, back_rs) = refs[16:20]
    refs = refs[20:]
    count = len(orders)
    if scatter:
        ins = refs[:count]
        refs = refs[count:]
        recv = [refs[i * stages : (i + 1) * stages] for i in range(count)]
        refs = refs[count * stages :]
        sums = [refs[i * (stages - 1) : (i + 1) * (stages - 1)] for i in range(count)]
        refs = refs[count * (stages - 1) :]
        send = [refs[i * (stages - 1) : (i + 1) * (stages - 1)] for i in range(count)]
        send_sem, recv_sem = refs[count * (stages - 1) :]
    agents, width = feat_ref.shape
    actions_all = wp_ref.shape[1]
    per_peer = ENV_AGENTS // env_devs
    per_device = ENV_DEV * per_peer
    inv_peers = 1.0 / (team_devs * agents // TEAMS - 1)
    agent_total = agents * team_devs * env_devs
    team, env = lax.axis_index("team"), lax.axis_index("env")
    mesh_id = pl.DeviceIdType.MESH
    team_peers = [((team + d) % team_devs, env) for d in range(1, team_devs)]
    env_peers = [(team, (env + d) % env_devs) for d in range(1, env_devs)]

    barrier = pltpu.get_barrier_semaphore()
    for peer in team_peers + env_peers:
        pl.semaphore_signal(barrier, inc=1, device_id=peer, device_id_type=mesh_id)

    def remote(source, target, send_one, recv_one, peer):
        copy = pltpu.make_async_remote_copy(
            src_ref=source,
            dst_ref=target,
            send_sem=send_one,
            recv_sem=recv_one,
            device_id=peer,
            device_id_type=mesh_id,
        )
        copy.start()
        return copy

    def iota(shape, dim):
        return lax.broadcasted_iota(jnp.int32, shape, dim)

    def team_exchange(source, target, send_one, recv_one):
        return [
            remote(source, target.at[d], send_one.at[d], recv_one.at[d], peer)
            for d, peer in enumerate(team_peers)
        ]

    def team_total(copies, source, target):
        total = source[...]
        for d, copy in enumerate(copies):
            copy.wait()
            total = total + target[d]
        return total

    team_col = col_ref[:, 0:1]

    def share(sums_all):
        total = jnp.where(team_col == 0.0, sums_all[0:1, :], 0.0)
        for t in range(1, TEAMS):
            total = jnp.where(team_col == float(t), sums_all[t : t + 1, :], total)
        return total

    features = feat_ref[...]
    team_row = lane_ref[0:1, :]
    sub = iota((8, agents), 0)
    mask_row = (sub.astype(jnp.float32) == team_row) & (sub < TEAMS)
    team_low = jnp.where(mask_row, 1.0, 0.0).astype(jnp.bfloat16)
    adv_row = lane_ref[3:4, :]
    adv_sum = jnp.sum(adv_row, axis=1, keepdims=True)
    adv_squares = jnp.sum(adv_row * adv_row, axis=1, keepdims=True)
    sub = iota((8, width), 0)
    part = matmul(team_low, features)
    part = jnp.where(sub == TEAMS, adv_sum, part)
    team_send[...] = jnp.where(sub == TEAMS + 1, adv_squares, part)
    pl.semaphore_wait(barrier, len(team_peers) + len(env_peers))
    flight = team_exchange(team_send, team_recv, team_ss, team_rs)

    own_part = matmul(features, wh_ref[...])
    env_row = lane_ref[1:2, :].astype(jnp.int32)
    key_row = (env_row // ENV_DEV % env_devs) * ENV_DEV + env_row % ENV_DEV
    keys_all = ENV_DEV * env_devs
    key_mask = jnp.where(iota((keys_all, agents), 0) == key_row, 1.0, 0.0)
    earlier = jnp.where(iota((agents, agents), 0) < iota((agents, agents), 1), 1.0, 0.0)
    ranks = matmul(key_mask.astype(jnp.bfloat16), earlier.astype(jnp.bfloat16))
    rank = jnp.sum(ranks * key_mask, axis=0, keepdims=True)
    slot = key_row * per_peer + rank.astype(jnp.int32)
    placing = jnp.where(iota((agents, agents), 0) == slot, 1.0, 0.0).astype(jnp.bfloat16)
    returns_row = jnp.broadcast_to(lane_ref[2:3, :], (8, agents)).astype(jnp.bfloat16)
    targets_row = times_trans(returns_row, placing)

    team_sums = team_total(flight, team_send, team_recv)
    sub = iota((8, agents), 0)
    tail = jnp.where(sub == 1, team_sums[TEAMS : TEAMS + 1, 0:1], targets_row)
    tail_send[...] = jnp.where(sub == 2, team_sums[TEAMS + 1 : TEAMS + 2, 0:1], tail)
    tail_recv[env] = tail_send[...]
    tail_flight = [
        remote(tail_send, tail_recv.at[env], tail_ss.at[d], tail_rs.at[d], peer)
        for d, peer in enumerate(env_peers)
    ]
    message = ((share(team_sums) - features.astype(jnp.float32)) * inv_peers).astype(jnp.bfloat16)
    hidden = jnp.tanh(own_part + matmul(message, wc_ref[...])).astype(jnp.bfloat16)
    outgoing = matmul(placing, hidden).reshape(env_devs, per_device, width)
    rows_send[...] = outgoing.astype(jnp.bfloat16)
    rows_recv[env] = rows_send[env]
    rows_flight = [
        remote(rows_send.at[peer[1]], rows_recv.at[env], rows_ss.at[d], rows_rs.at[d], peer)
        for d, peer in enumerate(env_peers)
    ]

    logits = matmul(hidden, wp_ref[...])
    raised = jnp.exp(logits)
    totals = jnp.sum(raised, axis=-1, keepdims=True)
    probs_all = raised / totals
    log_probs = logits - jnp.log(totals)
    lane = iota((agents, actions_all), 1).astype(jnp.float32)
    chosen = jnp.where(lane == col_ref[:, 1:2], 1.0, 0.0)
    log_chosen = jnp.sum(chosen * log_probs, axis=-1, keepdims=True)
    ratios = jnp.exp(log_chosen - col_ref[:, 2:3])
    for copy in tail_flight:
        copy.wait()
    adv_total = jnp.sum(tail_recv[:, 1, 0:1], axis=0, keepdims=True)
    adv_total_sq = jnp.sum(tail_recv[:, 2, 0:1], axis=0, keepdims=True)
    adv_mean = adv_total / agent_total
    adv_var = adv_total_sq / agent_total - adv_mean * adv_mean
    scaled = (col_ref[:, 3:4] - adv_mean) / jnp.sqrt(adv_var + NORM_EPS)
    delta_grad = -ratios * scaled + KL_WEIGHT * (ratios - 1.0)
    logit_grad = (delta_grad * (chosen - probs_all)).astype(jnp.bfloat16)
    policy_back = times_trans(logit_grad, wp_ref[...])
    policy_part = trans_times(hidden, logit_grad)
    target_rows = tail_recv[:, 0, :].astype(jnp.bfloat16)

    for copy in rows_flight:
        copy.wait()
    kept_items = []
    for item in range(ENV_DEV):
        here = slice(item * per_peer, (item + 1) * per_peer)
        rows_in = rows_recv[:, here, :].astype(jnp.float32).reshape(ENV_AGENTS, width)
        row_id = iota((ENV_AGENTS, env_devs), 0)
        pick = jnp.where(row_id // per_peer == iota((ENV_AGENTS, env_devs), 1), 1.0, 0.0)
        spread = matmul(pick.astype(jnp.bfloat16), target_rows)
        wanted = iota((ENV_AGENTS, agents), 0) % per_peer + item * per_peer + env * per_device
        keep = iota((ENV_AGENTS, agents), 1) == wanted
        targets = jnp.sum(jnp.where(keep, spread, 0.0), axis=1, keepdims=True)
        back, *kept = critic_item(
            rows_in, targets, gain_ref[...], wq_ref[...], wk_ref[...], wv_ref[...]
        )
        back = back.astype(jnp.float32).reshape(env_devs, per_peer, width)
        back_send[:, here, :] = back.astype(jnp.bfloat16)
        kept_items.append(kept)
    back_recv[env] = back_send[env]
    back_flight = [
        remote(back_send.at[peer[1]], back_recv.at[env], back_ss.at[d], back_rs.at[d], peer)
        for d, peer in enumerate(env_peers)
    ]

    def place(bit):
        if bit < team_bits:
            step = 1 << (team_bits - 1 - bit)
            mine = (team // step) % 2
            return mine, (team + (1 - 2 * mine) * step, env)
        step = 1 << (stages - 1 - bit)
        mine = (env // step) % 2
        return mine, (team, env + (1 - 2 * mine) * step)

    places = [place(bit) for bit in range(stages)]

    def start(i, stage):
        bit = orders[i][stage]
        axis = sum(1 for b in range(bit) if b not in orders[i][:stage])
        mine, peer = places[bit]
        before = (slice(None),) * axis
        if stage == 0:
            source = ins[i].at[before + (1 - mine,)]
        else:
            source = send[i][stage - 1]
            source[...] = sums[i][stage - 1][before + (1 - mine,)].astype(jnp.bfloat16)
        copy = remote(source, recv[i][stage], send_sem.at[i, stage], recv_sem.at[i, stage], peer)
        return copy, before + (mine,)

    pending = [None] * count

    def advance(i, stage):
        copy, kept = pending[i]
        copy.wait()
        held = ins[i] if stage == 0 else sums[i][stage - 1]
        total = held[kept].astype(jnp.float32) + recv[i][stage][...].astype(jnp.float32)
        if stage == stages - 1:
            outs[i][...] = total
        else:
            sums[i][stage][...] = total
            pending[i] = start(i, stage + 1)

    def emit(i, values):
        if not scatter:
            at = 0
            for value in values:
                outs[i][:, at : at + value.shape[1]] = value.astype(jnp.bfloat16)
                at += value.shape[1]
            return
        at = 0
        for value in values:
            cut = value.reshape(ins[i].shape[:-1] + (value.shape[1],)).astype(jnp.bfloat16)
            ins[i][..., at : at + value.shape[1]] = cut
            at += value.shape[1]
        pending[i] = start(i, 0)

    critic_parts = []
    for which in (1, 2):
        total = trans_times(kept_items[0][0], kept_items[0][which])
        for kept in kept_items[1:]:
            total = total + trans_times(kept[0], kept[which])
        critic_parts.append(total)
    emit(3, critic_parts)
    emit(2, [policy_part])

    for copy in back_flight:
        copy.wait()
    critic_grad = trans_times(placing, back_recv[...].reshape(agents, width))
    hidden_full = hidden.astype(jnp.float32)
    pre_grad = (policy_back + critic_grad) * (1.0 - hidden_full * hidden_full)
    pre_grad = pre_grad.astype(jnp.bfloat16)
    message_grad = times_trans(pre_grad, wc_ref[...])
    msg_send[...] = jnp.dot(
        team_low.astype(jnp.float32),
        message_grad,
        precision=lax.Precision.HIGHEST,
        preferred_element_type=jnp.float32,
    )
    flight = team_exchange(msg_send, msg_recv, msg_ss, msg_rs)
    emit(0, [trans_times(features, pre_grad)])
    emit(1, [trans_times(message, pre_grad)])
    if scatter:
        advance(3, 0)
        advance(2, 0)
    base = times_trans(pre_grad, wh_ref[...])
    message_sums = team_total(flight, msg_send, msg_recv)
    out_ref[...] = (base + (share(message_sums) - message_grad) * inv_peers).astype(jnp.bfloat16)
    if scatter:
        for stage in range(1, stages):
            for i in (0, 1):
                advance(i, stage - 1)
            for i in (3, 2):
                advance(i, stage)
        for i in (0, 1):
            advance(i, stages - 1)


def body(
    features,
    team_of,
    env_of,
    actions,
    old_logp,
    advantages,
    returns,
    w_hidden,
    w_comm,
    w_policy,
    norm_gain,
    w_query,
    w_key,
    w_value,
):
    agents, width = features.shape
    team_devs, env_devs = lax.axis_size("team"), lax.axis_size("env")
    devices = team_devs * env_devs
    team_bits, env_bits = log2(team_devs), log2(env_devs)
    stages = team_bits + env_bits
    full = jnp.float32
    zero = jnp.zeros_like(advantages)
    lanes = [team_of.astype(full), env_of.astype(full), returns.astype(full), advantages]
    lanes = jnp.stack(lanes + [zero] * 4, axis=0)
    columns = jnp.stack(
        [team_of.astype(full), actions.astype(full), old_logp, advantages] + [zero] * 4, axis=1
    )
    rows = width // devices
    scatter = width % devices == 0 and rows % 16 == 0
    widths = [width, width, w_policy.shape[1], 2 * width]
    team_order = list(range(team_bits))[::-1]
    env_order = list(range(team_bits, stages))[::-1]
    first = team_order + env_order
    second = team_order[:1] + env_order + team_order[1:]
    orders = [first, first, second, second]
    per_device = ENV_DEV * ENV_AGENTS // env_devs
    low = jnp.bfloat16
    dma = pltpu.SemaphoreType.DMA

    def both(shape, dtype, copies):
        return [pltpu.VMEM(shape, dtype), pltpu.VMEM((copies,) + shape, dtype)]

    trade = (env_devs, per_device, width)
    scratch = both((8, width), full, team_devs - 1) * 2
    scratch += [pltpu.VMEM(trade, low)] * 2
    scratch += both((8, agents), full, env_devs)
    scratch += [pltpu.VMEM(trade, low)] * 2
    scratch += [dma((team_devs - 1,))] * 4 + [dma((env_devs - 1,))] * 6
    if scatter:

        def left(columns_in, stage, dtype):
            return pltpu.VMEM((2,) * (stages - 1 - stage) + (rows, columns_in), dtype)

        scratch += [left(c, -1, low) for c in widths]
        scratch += [left(c, s, low) for c in widths for s in range(stages)]
        scratch += [left(c, s, full) for c in widths for s in range(stages - 1)]
        scratch += [left(c, s + 1, low) for c in widths for s in range(stages - 1)]
        scratch += [dma((len(widths), stages))] * 2
        out_parts = tuple(jax.ShapeDtypeStruct((rows, c), full) for c in widths)
    else:
        out_parts = tuple(jax.ShapeDtypeStruct((width, c), low) for c in widths)
    grad_input, *parts = pl.pallas_call(
        functools.partial(window_kernel, team_devs, env_devs, orders, scatter),
        out_shape=(jax.ShapeDtypeStruct((agents, width), low),) + out_parts,
        in_specs=[pl.BlockSpec(memory_space=pltpu.VMEM)] * 10,
        out_specs=(pl.BlockSpec(memory_space=pltpu.VMEM),) * 5,
        scratch_shapes=scratch,
        compiler_params=pltpu.CompilerParams(
            collective_id=0, has_side_effects=True, vmem_limit_bytes=52 * 1024 * 1024
        ),
        cost_estimate=pl.CostEstimate(
            flops=11_000_000_000, bytes_accessed=6_000_000, transcendentals=1_000_000
        ),
    )(
        features,
        lanes,
        columns,
        w_hidden,
        w_comm,
        w_policy,
        norm_gain[None, :],
        w_query,
        w_key,
        w_value[None, :],
    )
    if not scatter:
        parts = [
            lax.psum_scatter(p.astype(full), ("team", "env"), scatter_dimension=0, tiled=True)
            for p in parts
        ]
    grad_w_hidden, grad_w_comm, grad_w_policy, critic_sums = parts
    return (
        grad_input,
        grad_w_hidden,
        grad_w_comm,
        grad_w_policy,
        critic_sums[:, :width],
        critic_sums[:, width:],
    )


def solution(mesh):
    in_specs = (
        P(("team", "env"), None),
        P(("team", "env")),
        P(("team", "env")),
        P(("team", "env")),
        P(("team", "env")),
        P(("team", "env")),
        P(("team", "env")),
        P(),
        P(),
        P(),
        P(),
        P(),
        P(),
        P(),
    )
    out_specs = (
        P(("team", "env"), None),
        P(("team", "env"), None),
        P(("team", "env"), None),
        P(("team", "env"), None),
        P(("team", "env"), None),
        P(("team", "env"), None),
    )
    return jax.shard_map(body, mesh=mesh, in_specs=in_specs, out_specs=out_specs, check_vma=False)
```

time: 331 us -> 79 us (0.24)
  waiting for transfers between devices: 143 us -> 0 us
  Pallas kernels: 0 us -> 69.3 us
  blocking collectives: 54.6 us -> 0 us
  matrix products: 40.6 us -> 0 us
  local copies, waits for them, and re-layouts: 39.8 us -> 8.64 us
  starting transfers between devices: 17.5 us -> 0 us
  other arithmetic: 16.6 us -> 0.01 us
  between operations: 17.1 us -> 0.7 us
    unnamed x2 -> x0, waiting for transfers between devices: 134 us -> none
    pallas_call x0 -> x1, Pallas kernels: none -> 69.3 us  [body(): pl.pallas_call(functools.partial(window_kernel, team_devs, env_devs, orde...]
    psum x3 -> x0, blocking collectives: 54.6 us -> none  [the longest x1 42.2 us: body(): lax.psum((jnp.sum(advantages), jnp.sum(advantages * advantages)), ('team'...]
    dot_general x25 -> x0, matrix products: 40.6 us -> none  [the longest x6 8.25 us: trans_times(): lax.dot_general(left_side, right_side, (((0,), (0,)), ((), ())), preferre...]
    all_to_all x3 -> x0, starting transfers between devices: 17.4 us -> none  [the longest x1 7.28 us: body(): lax.all_to_all(outgoing_targets, 'env', split_axis=1, concat_axis=1, tile...]
    all_to_all x3 -> x0, waiting for transfers between devices: 9.12 us -> none  [the longest x1 9.11 us: body(): lax.all_to_all(input_grad.reshape(item_count, env_devs, per_peer, model_w...]
    reshape x8 -> x0, local copies, waits for them, and re-layouts: 8.34 us -> none  [the longest x2 2.99 us: critic_pass(): key_heads = key_rows.reshape(head_shape)]
    gather x3 -> x0, local copies, waits for them, and re-layouts: 7.58 us -> none  [the longest x1 3.64 us: body(): outgoing_targets = returns[ordering].reshape(ENV_DEV, env_devs, per_peer)]
  transfers between devices with their start and end apart: 4 -> 0, of which waited for: 2 -> 0; matrix products, arithmetic and copies ran while one was open for 5% -> 0% of each run, Pallas kernels for 0% -> 0%
where the time goes in v2:
time: 79 us; the launch traced here: 78.7 us
  Pallas kernels  69.3 us (88%)
  local copies, waits for them, and re-layouts  8.64 us (11%)
    pallas_call x1, Pallas kernels, body(): pl.pallas_call(functools.partial(window_kernel, team_devs, env_devs, orde...  69.3 us
    unnamed x24, local copies, waits for them, and re-layouts  7.82 us

profile of v2, /device:TPU:0, one launch (start us, length us, event | category | flops | bytes accessed | tf_op | source)
XLA Modules:
  0.0 78.7 jit_solution(2440209268424790325)
XLA Ops:
  0.6 0.0 copy-start.6
  0.6 0.7 copy-done.6
  1.3 0.0 copy-start.7
  1.3 0.7 copy-done.7
  2.0 0.0 copy-start.8
  2.0 0.7 copy-done.8
  2.7 0.0 copy-start.9
  2.7 0.7 copy-done.9
  3.4 0.7 copy-done.4
  4.0 0.0 copy-done.5
  4.1 0.0 copy-start.1
  4.1 0.0 copy-start.2
  4.2 0.0 copy-start.3
  4.2 0.1 copy.24.refs_2_
  4.3 0.7 copy-done.1
  5.0 0.0 copy-done.2
  5.0 0.0 copy-done.3
  5.0 1.0 %copy-done = bf16[512,512]{1,0:T(8,128)(2,1)S(1)} copy-done((bf16[512,512]{1,0:T(8,128)(2,1)S(1)}, bf16[512,512]{1,0:T(8,128)(2,1)}, u32[]{:S(2)}) %copy-start) | copy-done | bytes 524312
  6.1 69.3 %shard_map.181 = (bf16[512,512]{1,0:T(8,128)(2,1)S(1)}, f32[16,512]{1,0:T(8,128)S(1)}, f32[16,512]{1,0:T(8,128)S(1)}, f32[16,128]{1,0:T(8,128)S(1)}, f32[16,1024]{1,0:T(8,128)S(1)}) custom-call(bf16[512,512]{1,0:T(8,128)(2,1)S(1)} %copy-done, f32[8,512]{1,0:T(8,128)S(1)} %stack.45.refs_1_, f32[512,8]{1,0:T(8,128)S(1)} %copy.24.refs_2_, ...), custom_call_target="tpu_custom_call" | custom-call | flops 11000000512 | bytes 6000000 | tf_op jit(solution)/shard_map/pallas_call | solution.py:416
  75.4 0.6 fusion
  76.0 0.8 %copy.29 = bf16[512,512]{1,0:T(8,128)(2,1)} copy(bf16[512,512]{1,0:T(8,128)(2,1)S(1)} %get-tuple-element.24) | data formatting | bytes 1048576
  76.8 0.6 copy.30
  77.4 0.6 copy.31
  78.1 0.6 copy.32
  (11 shorter events, 0.1 us)
Async XLA Ops:
  0.6 0.7 copy-start.6
  1.3 0.7 copy-start.7
  2.0 0.7 copy-start.8
  2.7 0.7 copy-start.9
  3.4 0.7 copy-start.4
  3.4 0.7 copy-start.5
  4.1 0.9 %copy-start.1 = (bf16[512,128]{1,0:T(8,128)(2,1)S(1)}, bf16[512,128]{1,0:T(8,128)(2,1)}, u32[]{:S(2)}) copy-start(bf16[512,128]{1,0:T(8,128)(2,1)} %refs_5_.1) | copy-start | bytes 393220
  4.1 0.9 %copy-start.2 = (f32[512]{0:T(512)S(1)}, f32[512]{0:T(512)}, u32[]{:S(2)}) copy-start(f32[512]{0:T(512)} %param.24) | copy-start | bytes 6148
  4.2 0.9 %copy-start.3 = (f32[512]{0:T(512)S(1)}, f32[512]{0:T(512)}, u32[]{:S(2)}) copy-start(f32[512]{0:T(512)} %param.27) | copy-start | bytes 6148
  5.0 1.0 %copy-start = (bf16[512,512]{1,0:T(8,128)(2,1)S(1)}, bf16[512,512]{1,0:T(8,128)(2,1)}, u32[]{:S(2)}) copy-start(bf16[512,512]{1,0:T(8,128)(2,1)} %refs_0_.1) | copy-start | bytes 1572868

commit v3 on v2

--- a/solution.py
+++ b/solution.py
@@ -97,9 +97,19 @@
 def window_kernel(team_devs, env_devs, orders, scatter, *refs):
     team_bits, env_bits = log2(team_devs), log2(env_devs)
     stages = team_bits + env_bits
-    (feat_ref, lane_ref, col_ref, wh_ref, wc_ref, wp_ref, gain_ref, wq_ref, wk_ref, wv_ref) = refs[:10]
-    out_ref, outs = refs[10], refs[11:15]
-    refs = refs[15:]
+    feat_ref, wh_ref, wc_ref, wp_ref, gain_ref, wq_ref, wk_ref, wv_ref = refs[:8]
+    agent_hbm, out_ref, parts_ref = refs[8:14], refs[14], refs[15]
+    agent_refs, agent_sem = refs[16:22], refs[22]
+    refs = refs[23:]
+    loads = [
+        pltpu.make_async_copy(source, target, agent_sem.at[i])
+        for i, (source, target) in enumerate(zip(agent_hbm, agent_refs))
+    ]
+    for load in loads:
+        load.start()
+    actions_width, model_width = wp_ref.shape[1], wp_ref.shape[0]
+    edges = [0, model_width, 2 * model_width, 2 * model_width + actions_width]
+    edges.append(edges[-1] + 2 * model_width)
     (team_send, team_recv, msg_send, msg_recv, rows_send, rows_recv) = refs[:6]
     (tail_send, tail_recv, back_send, back_recv) = refs[6:10]
     (team_ss, team_rs, msg_ss, msg_rs, rows_ss, rows_rs) = refs[10:16]
@@ -158,20 +168,21 @@
             total = total + target[d]
         return total
 
-    team_col = col_ref[:, 0:1]
-
     def share(sums_all):
         total = jnp.where(team_col == 0.0, sums_all[0:1, :], 0.0)
         for t in range(1, TEAMS):
             total = jnp.where(team_col == float(t), sums_all[t : t + 1, :], total)
         return total
 
+    for load in loads:
+        load.wait()
+    team_ref, env_ref, action_ref, logp_ref, adv_ref, returns_ref = agent_refs
     features = feat_ref[...]
-    team_row = lane_ref[0:1, :]
+    team_row = team_ref[...].astype(jnp.float32)
     sub = iota((8, agents), 0)
     mask_row = (sub.astype(jnp.float32) == team_row) & (sub < TEAMS)
     team_low = jnp.where(mask_row, 1.0, 0.0).astype(jnp.bfloat16)
-    adv_row = lane_ref[3:4, :]
+    adv_row = adv_ref[...]
     adv_sum = jnp.sum(adv_row, axis=1, keepdims=True)
     adv_squares = jnp.sum(adv_row * adv_row, axis=1, keepdims=True)
     sub = iota((8, width), 0)
@@ -181,8 +192,14 @@
     pl.semaphore_wait(barrier, len(team_peers) + len(env_peers))
     flight = team_exchange(team_send, team_recv, team_ss, team_rs)
 
+    diagonal = iota((agents, agents), 0) == iota((agents, agents), 1)
+
+    def column(row):
+        return jnp.sum(jnp.where(diagonal, row, 0.0), axis=1, keepdims=True)
+
+    team_col = column(team_row)
     own_part = matmul(features, wh_ref[...])
-    env_row = lane_ref[1:2, :].astype(jnp.int32)
+    env_row = env_ref[...]
     key_row = (env_row // ENV_DEV % env_devs) * ENV_DEV + env_row % ENV_DEV
     keys_all = ENV_DEV * env_devs
     key_mask = jnp.where(iota((keys_all, agents), 0) == key_row, 1.0, 0.0)
@@ -191,7 +208,7 @@
     rank = jnp.sum(ranks * key_mask, axis=0, keepdims=True)
     slot = key_row * per_peer + rank.astype(jnp.int32)
     placing = jnp.where(iota((agents, agents), 0) == slot, 1.0, 0.0).astype(jnp.bfloat16)
-    returns_row = jnp.broadcast_to(lane_ref[2:3, :], (8, agents)).astype(jnp.bfloat16)
+    returns_row = jnp.broadcast_to(returns_ref[...], (8, agents)).astype(jnp.bfloat16)
     targets_row = times_trans(returns_row, placing)
 
     team_sums = team_total(flight, team_send, team_recv)
@@ -208,10 +225,23 @@
     outgoing = matmul(placing, hidden).reshape(env_devs, per_device, width)
     rows_send[...] = outgoing.astype(jnp.bfloat16)
     rows_recv[env] = rows_send[env]
-    rows_flight = [
-        remote(rows_send.at[peer[1]], rows_recv.at[env], rows_ss.at[d], rows_rs.at[d], peer)
-        for d, peer in enumerate(env_peers)
-    ]
+    groups = ENV_DEV if per_peer % 16 == 0 else 1
+    group_rows = per_device // groups
+
+    def trade(group, source, target, send_one, recv_one):
+        here = pl.ds(group * group_rows, group_rows)
+        return [
+            remote(
+                source.at[peer[1], here],
+                target.at[env, here],
+                send_one.at[group, d],
+                recv_one.at[group, d],
+                peer,
+            )
+            for d, peer in enumerate(env_peers)
+        ]
+
+    rows_flight = [trade(g, rows_send, rows_recv, rows_ss, rows_rs) for g in range(groups)]
 
     logits = matmul(hidden, wp_ref[...])
     raised = jnp.exp(logits)
@@ -219,26 +249,28 @@
     probs_all = raised / totals
     log_probs = logits - jnp.log(totals)
     lane = iota((agents, actions_all), 1).astype(jnp.float32)
-    chosen = jnp.where(lane == col_ref[:, 1:2], 1.0, 0.0)
+    chosen = jnp.where(lane == column(action_ref[...].astype(jnp.float32)), 1.0, 0.0)
     log_chosen = jnp.sum(chosen * log_probs, axis=-1, keepdims=True)
-    ratios = jnp.exp(log_chosen - col_ref[:, 2:3])
+    ratios = jnp.exp(log_chosen - column(logp_ref[...]))
     for copy in tail_flight:
         copy.wait()
     adv_total = jnp.sum(tail_recv[:, 1, 0:1], axis=0, keepdims=True)
     adv_total_sq = jnp.sum(tail_recv[:, 2, 0:1], axis=0, keepdims=True)
     adv_mean = adv_total / agent_total
     adv_var = adv_total_sq / agent_total - adv_mean * adv_mean
-    scaled = (col_ref[:, 3:4] - adv_mean) / jnp.sqrt(adv_var + NORM_EPS)
+    scaled = (column(adv_row) - adv_mean) / jnp.sqrt(adv_var + NORM_EPS)
     delta_grad = -ratios * scaled + KL_WEIGHT * (ratios - 1.0)
     logit_grad = (delta_grad * (chosen - probs_all)).astype(jnp.bfloat16)
     policy_back = times_trans(logit_grad, wp_ref[...])
     policy_part = trans_times(hidden, logit_grad)
     target_rows = tail_recv[:, 0, :].astype(jnp.bfloat16)
 
-    for copy in rows_flight:
-        copy.wait()
     kept_items = []
+    back_flight = []
     for item in range(ENV_DEV):
+        if item < groups:
+            for copy in rows_flight[item]:
+                copy.wait()
         here = slice(item * per_peer, (item + 1) * per_peer)
         rows_in = rows_recv[:, here, :].astype(jnp.float32).reshape(ENV_AGENTS, width)
         row_id = iota((ENV_AGENTS, env_devs), 0)
@@ -253,11 +285,10 @@
         back = back.astype(jnp.float32).reshape(env_devs, per_peer, width)
         back_send[:, here, :] = back.astype(jnp.bfloat16)
         kept_items.append(kept)
+        if groups > 1 or item == ENV_DEV - 1:
+            group = item if groups > 1 else 0
+            back_flight += trade(group, back_send, back_recv, back_ss, back_rs)
     back_recv[env] = back_send[env]
-    back_flight = [
-        remote(back_send.at[peer[1]], back_recv.at[env], back_ss.at[d], back_rs.at[d], peer)
-        for d, peer in enumerate(env_peers)
-    ]
 
     def place(bit):
         if bit < team_bits:
@@ -291,16 +322,16 @@
         held = ins[i] if stage == 0 else sums[i][stage - 1]
         total = held[kept].astype(jnp.float32) + recv[i][stage][...].astype(jnp.float32)
         if stage == stages - 1:
-            outs[i][...] = total
+            parts_ref[:, edges[i] : edges[i + 1]] = total
         else:
             sums[i][stage][...] = total
             pending[i] = start(i, stage + 1)
 
     def emit(i, values):
         if not scatter:
-            at = 0
+            at = edges[i]
             for value in values:
-                outs[i][:, at : at + value.shape[1]] = value.astype(jnp.bfloat16)
+                parts_ref[:, at : at + value.shape[1]] = value.astype(jnp.bfloat16)
                 at += value.shape[1]
             return
         at = 0
@@ -373,12 +404,6 @@
     team_bits, env_bits = log2(team_devs), log2(env_devs)
     stages = team_bits + env_bits
     full = jnp.float32
-    zero = jnp.zeros_like(advantages)
-    lanes = [team_of.astype(full), env_of.astype(full), returns.astype(full), advantages]
-    lanes = jnp.stack(lanes + [zero] * 4, axis=0)
-    columns = jnp.stack(
-        [team_of.astype(full), actions.astype(full), old_logp, advantages] + [zero] * 4, axis=1
-    )
     rows = width // devices
     scatter = width % devices == 0 and rows % 16 == 0
     widths = [width, width, w_policy.shape[1], 2 * width]
@@ -395,11 +420,16 @@
         return [pltpu.VMEM(shape, dtype), pltpu.VMEM((copies,) + shape, dtype)]
 
     trade = (env_devs, per_device, width)
-    scratch = both((8, width), full, team_devs - 1) * 2
+    agent_inputs = [team_of, env_of, actions, old_logp, advantages, returns.astype(full)]
+    agent_inputs = [value[None, :] for value in agent_inputs]
+    scratch = [pltpu.VMEM(value.shape, value.dtype) for value in agent_inputs]
+    scratch += [dma((len(agent_inputs),))]
+    scratch += both((8, width), full, team_devs - 1) * 2
     scratch += [pltpu.VMEM(trade, low)] * 2
     scratch += both((8, agents), full, env_devs)
     scratch += [pltpu.VMEM(trade, low)] * 2
-    scratch += [dma((team_devs - 1,))] * 4 + [dma((env_devs - 1,))] * 6
+    scratch += [dma((team_devs - 1,))] * 4 + [dma((ENV_DEV, env_devs - 1))] * 2
+    scratch += [dma((env_devs - 1,))] * 2 + [dma((ENV_DEV, env_devs - 1))] * 2
     if scatter:
 
         def left(columns_in, stage, dtype):
@@ -410,25 +440,23 @@
         scratch += [left(c, s, full) for c in widths for s in range(stages - 1)]
         scratch += [left(c, s + 1, low) for c in widths for s in range(stages - 1)]
         scratch += [dma((len(widths), stages))] * 2
-        out_parts = tuple(jax.ShapeDtypeStruct((rows, c), full) for c in widths)
+        out_parts = jax.ShapeDtypeStruct((rows, sum(widths)), full)
     else:
-        out_parts = tuple(jax.ShapeDtypeStruct((width, c), low) for c in widths)
-    grad_input, *parts = pl.pallas_call(
+        out_parts = jax.ShapeDtypeStruct((width, sum(widths)), low)
+    grad_input, parts = pl.pallas_call(
         functools.partial(window_kernel, team_devs, env_devs, orders, scatter),
-        out_shape=(jax.ShapeDtypeStruct((agents, width), low),) + out_parts,
-        in_specs=[pl.BlockSpec(memory_space=pltpu.VMEM)] * 10,
-        out_specs=(pl.BlockSpec(memory_space=pltpu.VMEM),) * 5,
+        out_shape=(jax.ShapeDtypeStruct((agents, width), low), out_parts),
+        in_specs=[pl.BlockSpec(memory_space=pltpu.VMEM)] * 8 + [pl.BlockSpec(memory_space=pl.ANY)] * 6,
+        out_specs=(pl.BlockSpec(memory_space=pltpu.VMEM),) * 2,
         scratch_shapes=scratch,
         compiler_params=pltpu.CompilerParams(
-            collective_id=0, has_side_effects=True, vmem_limit_bytes=52 * 1024 * 1024
+            collective_id=0, has_side_effects=True, vmem_limit_bytes=60 * 1024 * 1024
         ),
         cost_estimate=pl.CostEstimate(
             flops=11_000_000_000, bytes_accessed=6_000_000, transcendentals=1_000_000
         ),
     )(
         features,
-        lanes,
-        columns,
         w_hidden,
         w_comm,
         w_policy,
@@ -436,21 +464,16 @@
         w_query,
         w_key,
         w_value[None, :],
+        *agent_inputs,
     )
     if not scatter:
-        parts = [
-            lax.psum_scatter(p.astype(full), ("team", "env"), scatter_dimension=0, tiled=True)
-            for p in parts
-        ]
-    grad_w_hidden, grad_w_comm, grad_w_policy, critic_sums = parts
-    return (
-        grad_input,
-        grad_w_hidden,
-        grad_w_comm,
-        grad_w_policy,
-        critic_sums[:, :width],
-        critic_sums[:, width:],
-    )
+        parts = lax.psum_scatter(
+            parts.astype(full), ("team", "env"), scatter_dimension=0, tiled=True
+        )
+    edges = [0]
+    for wide in (width, width, w_policy.shape[1], width, width):
+        edges.append(edges[-1] + wide)
+    return (grad_input, *[parts[:, a:b] for a, b in zip(edges[:-1], edges[1:])])
 
 
 def solution(mesh):

time: 79 us -> 71.7 us (0.908)
  Pallas kernels: 69.3 us -> 64.8 us
  local copies, waits for them, and re-layouts: 8.64 us -> 5.29 us
    unnamed x24 -> x3, local copies, waits for them, and re-layouts: 7.82 us -> 2.54 us
    pallas_call x1, Pallas kernels: 69.3 us -> 64.8 us  [body(): pl.pallas_call(functools.partial(window_kernel, team_devs, env_devs, orde...]
    slice x1 -> x2, local copies, waits for them, and re-layouts: 0.63 us -> 2.75 us  [body(): return (grad_input, *[parts[:, a:b] for a, b in zip(edges[:-1], edges[1:])])]
where the time goes in v3:
time: 71.7 us; the launch traced here: 71.3 us
  Pallas kernels  64.8 us (90%)
  local copies, waits for them, and re-layouts  5.29 us (7%)
    pallas_call x1, Pallas kernels, body(): pl.pallas_call(functools.partial(window_kernel, team_devs, env_devs, orde...  64.8 us
    slice x2, local copies, waits for them, and re-layouts, body(): return (grad_input, *[parts[:, a:b] for a, b in zip(edges[:-1], edges[1:])])  2.75 us
    unnamed x3, local copies, waits for them, and re-layouts  2.54 us

profile of v3, /device:TPU:0, one launch (start us, length us, event | category | flops | bytes accessed | tf_op | source)
XLA Modules:
  0.0 71.3 jit_solution(2895982335699746688)
XLA Ops:
  0.6 0.0 copy-start
  0.6 0.7 copy-done
  1.3 0.6 broadcast_in_dim.35
  1.9 64.8 %shard_map.181 = (bf16[512,512]{1,0:T(8,128)(2,1)}, f32[16,2176]{1,0:T(8,128)}) custom-call(bf16[512,512]{1,0:T(8,128)(2,1)} %refs_0_.1, bf16[512,512]{1,0:T(8,128)(2,1)} %refs_1_.1, bf16[512,512]{1,0:T(8,128)(2,1)} %refs_2_.1, bf16[512,128]{1,0:T(8,128)(2,1)} %refs_3_.1, f32[1,512]{1,0:T(1,128)} %bitcast.9, bf16[512,512]{1,0:T(8,128)(2,1)} %refs_5_.1, ...), custom_call_target="tpu_custom_call" | custom-call | flops 11000000512 | bytes 6000000 | tf_op jit(solution)/shard_map/pallas_call | solution.py:446
  66.7 1.3 %slice.17 = f32[16,128]{1,0:T(8,128)} slice(f32[16,2176]{1,0:T(8,128)} %get-tuple-element.9), slice={[0:16], [1024:1152]} | slice | bytes 16384 | tf_op jit(solution)/shard_map/slice | solution.py:476
  68.0 1.5 %fusion = (f32[16,512]{1,0:T(8,128)}, f32[16,512]{1,0:T(8,128)}, f32[16,512]{1,0:T(8,128)}, f32[16,512]{1,0:T(8,128)}) fusion(f32[16,2176]{1,0:T(8,128)} %get-tuple-element.9), kind=kLoop, calls=%fused_computation | loop fusion | bytes 262144 | tf_op jit(solution)/shard_map/slice | solution.py:476
  69.5 1.9 %copy.21 = bf16[512,512]{1,0:T(8,128)(2,1)} copy(bf16[512,512]{1,0:T(8,128)(2,1)} %get-tuple-element.20) | data formatting | bytes 1048576
Async XLA Ops:
  0.6 0.7 copy-start

commit v4 on v3

--- a/solution.py
+++ b/solution.py
@@ -97,10 +97,11 @@
 def window_kernel(team_devs, env_devs, orders, scatter, *refs):
     team_bits, env_bits = log2(team_devs), log2(env_devs)
     stages = team_bits + env_bits
-    feat_ref, wh_ref, wc_ref, wp_ref, gain_ref, wq_ref, wk_ref, wv_ref = refs[:8]
-    agent_hbm, out_ref, parts_ref = refs[8:14], refs[14], refs[15]
-    agent_refs, agent_sem = refs[16:22], refs[22]
-    refs = refs[23:]
+    agent_hbm, out_ref, parts_ref = refs[:14], refs[14], refs[15]
+    agent_refs, agent_sem = refs[16:30], refs[30]
+    refs = refs[31:]
+    team_ref, env_ref, action_ref, logp_ref, adv_ref, returns_ref, feat_ref = agent_refs[:7]
+    wh_ref, wc_ref, wp_ref, gain_ref, wq_ref, wk_ref, wv_ref = agent_refs[7:]
     loads = [
         pltpu.make_async_copy(source, target, agent_sem.at[i])
         for i, (source, target) in enumerate(zip(agent_hbm, agent_refs))
@@ -174,9 +175,8 @@
             total = jnp.where(team_col == float(t), sums_all[t : t + 1, :], total)
         return total
 
-    for load in loads:
+    for load in loads[:7]:
         load.wait()
-    team_ref, env_ref, action_ref, logp_ref, adv_ref, returns_ref = agent_refs
     features = feat_ref[...]
     team_row = team_ref[...].astype(jnp.float32)
     sub = iota((8, agents), 0)
@@ -192,6 +192,8 @@
     pl.semaphore_wait(barrier, len(team_peers) + len(env_peers))
     flight = team_exchange(team_send, team_recv, team_ss, team_rs)
 
+    for load in loads[7:]:
+        load.wait()
     diagonal = iota((agents, agents), 0) == iota((agents, agents), 1)
 
     def column(row):
@@ -422,6 +424,8 @@
     trade = (env_devs, per_device, width)
     agent_inputs = [team_of, env_of, actions, old_logp, advantages, returns.astype(full)]
     agent_inputs = [value[None, :] for value in agent_inputs]
+    agent_inputs += [features, w_hidden, w_comm, w_policy, norm_gain[None, :]]
+    agent_inputs += [w_query, w_key, w_value[None, :]]
     scratch = [pltpu.VMEM(value.shape, value.dtype) for value in agent_inputs]
     scratch += [dma((len(agent_inputs),))]
     scratch += both((8, width), full, team_devs - 1) * 2
@@ -446,26 +450,16 @@
     grad_input, parts = pl.pallas_call(
         functools.partial(window_kernel, team_devs, env_devs, orders, scatter),
         out_shape=(jax.ShapeDtypeStruct((agents, width), low), out_parts),
-        in_specs=[pl.BlockSpec(memory_space=pltpu.VMEM)] * 8 + [pl.BlockSpec(memory_space=pl.ANY)] * 6,
+        in_specs=[pl.BlockSpec(memory_space=pltpu.HBM)] * 14,
         out_specs=(pl.BlockSpec(memory_space=pltpu.VMEM),) * 2,
         scratch_shapes=scratch,
         compiler_params=pltpu.CompilerParams(
-            collective_id=0, has_side_effects=True, vmem_limit_bytes=60 * 1024 * 1024
+            collective_id=0, has_side_effects=True, vmem_limit_bytes=56 * 1024 * 1024
         ),
         cost_estimate=pl.CostEstimate(
             flops=11_000_000_000, bytes_accessed=6_000_000, transcendentals=1_000_000
         ),
-    )(
-        features,
-        w_hidden,
-        w_comm,
-        w_policy,
-        norm_gain[None, :],
-        w_query,
-        w_key,
-        w_value[None, :],
-        *agent_inputs,
-    )
+    )(*agent_inputs)
     if not scatter:
         parts = lax.psum_scatter(
             parts.astype(full), ("team", "env"), scatter_dimension=0, tiled=True

time: 71.7 us -> 70 us (0.976)
  Pallas kernels: 64.8 us -> 63.2 us
    pallas_call x1, Pallas kernels: 64.8 us -> 63.2 us  [body(): pl.pallas_call(functools.partial(window_kernel, team_devs, env_devs, orde...]
where the time goes in v4:
time: 70 us; the launch traced here: 69.7 us
  Pallas kernels  63.2 us (90%)
  local copies, waits for them, and re-layouts  5.29 us (8%)
    pallas_call x1, Pallas kernels, body(): pl.pallas_call(functools.partial(window_kernel, team_devs, env_devs, orde...  63.2 us
    slice x2, local copies, waits for them, and re-layouts, body(): return (grad_input, *[parts[:, a:b] for a, b in zip(edges[:-1], edges[1:])])  2.75 us
    unnamed x3, local copies, waits for them, and re-layouts  2.54 us

profile of v4, /device:TPU:0, one launch (start us, length us, event | category | flops | bytes accessed | tf_op | source)
XLA Modules:
  0.0 69.7 jit_solution(7823458815921197488)
XLA Ops:
  0.6 0.0 copy-start
  0.6 0.7 copy-done
  1.3 0.6 broadcast_in_dim.35
  1.9 63.2 %shard_map.181 = (bf16[512,512]{1,0:T(8,128)(2,1)}, f32[16,2176]{1,0:T(8,128)}) custom-call(s32[1,512]{1,0:T(1,128)} %bitcast.9, s32[1,512]{1,0:T(1,128)} %bitcast.10, s32[1,512]{1,0:T(1,128)} %bitcast.11, f32[1,512]{1,0:T(1,128)} %bitcast.12, f32[1,512]{1,0:T(1,128)} %bitcast.13, f32[1,512]{1,0:T(1,128)} %bitcast.8, bf16[512,512]{1,0:T(8,128)(2,1)} %refs_6_.1, ...), custom_call_target="tpu_custom_call" | custom-call | flops 11000000512 | bytes 6000000 | tf_op jit(solution)/shard_map/pallas_call | solution.py:450
  65.1 1.3 %slice.17 = f32[16,128]{1,0:T(8,128)} slice(f32[16,2176]{1,0:T(8,128)} %get-tuple-element.9), slice={[0:16], [1024:1152]} | slice | bytes 16384 | tf_op jit(solution)/shard_map/slice | solution.py:470
  66.4 1.5 %fusion = (f32[16,512]{1,0:T(8,128)}, f32[16,512]{1,0:T(8,128)}, f32[16,512]{1,0:T(8,128)}, f32[16,512]{1,0:T(8,128)}) fusion(f32[16,2176]{1,0:T(8,128)} %get-tuple-element.9), kind=kLoop, calls=%fused_computation | loop fusion | bytes 262144 | tf_op jit(solution)/shard_map/slice | solution.py:470
  67.9 1.9 %copy.21 = bf16[512,512]{1,0:T(8,128)(2,1)} copy(bf16[512,512]{1,0:T(8,128)(2,1)} %get-tuple-element.20) | data formatting | bytes 1048576
Async XLA Ops:
  0.6 0.7 copy-start
